TPU v7x, 128 devices: a whole 4x4x4 slice. The times are simulated.
128 devices in a mesh: pair: 2 (over y_lo), vocab: 8 (over x, core), tok: 8 (over y_hi, z).
Axes of the slice: x: 4, y: 4 (y_hi: 2, y_lo: 2; y = y_hi * 2 + y_lo), z: 4, core: 2. Of those that a mesh axis runs over, the one named last changes fastest.
Arguments:
- teacher_hidden: bfloat16 [512, 4608], P(('pair', 'vocab', 'tok')), may hold values from -64 to 64
- teacher_gain: float32 [4608], replicated, may hold values from 0.1 to 1.9
- teacher_weight: bfloat16 [4608, 64, 2, 1024], P(None, ('vocab', 'tok'), 'pair'), may hold values from -4 to 4
- student_hidden: bfloat16 [512, 3584], P(('vocab', 'tok'), 'pair'), may hold values from -64 to 64
- student_gain: float32 [3584], P('pair'), may hold values from 0.1 to 1.9
- student_weight: bfloat16 [3584, 131072], P('pair', ('vocab', 'tok')), may hold values from -4 to 4
- token_weight: float32 [512], P('pair'), may hold values from 256 to 2048
Outputs:
- d_hidden: float32 [512, 3584], P(('vocab', 'tok'), 'pair')
- d_weight: bfloat16 [3584, 131072], P('pair', ('vocab', 'tok'))
All inputs are finite; a program needn't handle non-finite values.
Results may differ from a plain program's by a relative error of at most 0.0097.
Values may be sent and summed in bfloat16 or wider, within the bound.
A program may use at most 128 MiB of HBM per device.

v0:
```python
import jax
import jax.numpy as jnp
from jax import lax
from jax.sharding import PartitionSpec as P

DS = 3584


EPS = 1e-06
CAP = 30.0


def softcap(values):
    return CAP * jnp.tanh(values / CAP)


def teacher_norm_rows(rows, teacher_gain):
    values = rows.astype(jnp.float32)
    scale = lax.rsqrt(jnp.mean(values * values, axis=-1, keepdims=True) + EPS)
    return (values * scale * teacher_gain).astype(jnp.bfloat16)


def per_device(
    teacher_hidden,
    teacher_gain,
    teacher_weight,
    student_hidden,
    student_gain,
    student_weight,
    token_weight,
):
    head_t = teacher_weight.reshape(teacher_weight.shape[0], -1)
    normed_t = teacher_norm_rows(teacher_hidden, teacher_gain)
    teach_z = softcap(
        jnp.dot(
            lax.all_gather(normed_t, ("pair", "vocab", "tok"), axis=0, tiled=True),
            head_t,
            preferred_element_type=jnp.float32,
        )
    )
    stud_x = student_hidden.astype(jnp.float32)
    squares = lax.psum(jnp.sum(stud_x * stud_x, axis=-1), "pair")
    stud_r = lax.rsqrt(squares / DS + EPS)[:, None]
    normed_s = (stud_x * stud_r * student_gain).astype(jnp.bfloat16)
    gathered_s = lax.all_gather(normed_s, ("vocab", "tok"), axis=0, tiled=True)
    rows = gathered_s
    stud_z = softcap(
        lax.psum_scatter(
            jnp.dot(rows, student_weight, preferred_element_type=jnp.float32),
            "pair",
            scatter_dimension=0,
            tiled=True,
        )
    )
    stud_e = jnp.exp(stud_z)
    teach_e = jnp.exp(teach_z)
    teach_total = lax.psum(jnp.sum(teach_e, axis=-1), ("pair", "vocab", "tok"))
    probs_t = (teach_e / teach_total[:, None]).astype(jnp.bfloat16)
    slab = lax.all_to_all(probs_t, "pair", split_axis=0, concat_axis=1, tiled=True)
    stud_total = lax.psum(jnp.sum(stud_e, axis=-1), ("vocab", "tok"))
    stud_p = stud_e / stud_total[:, None]
    slope = 1.0 - (stud_z / CAP) ** 2
    logit_grad = (token_weight[:, None] * (stud_p - slab.astype(jnp.float32)) * slope).astype(
        jnp.bfloat16
    )
    grads_all = lax.all_gather(logit_grad, "pair", axis=0, tiled=True)
    d_weight = lax.dot_general(
        gathered_s, grads_all, (((0,), (0,)), ((), ())), preferred_element_type=jnp.float32
    ).astype(jnp.bfloat16)
    rows = grads_all
    d_normed = lax.psum_scatter(
        lax.dot_general(
            rows, student_weight, (((1,), (1,)), ((), ())), preferred_element_type=jnp.float32
        ),
        ("vocab", "tok"),
        scatter_dimension=0,
        tiled=True,
    )
    scaled = student_gain * d_normed
    inner = lax.psum(jnp.sum(stud_x * scaled, axis=-1), "pair")[:, None]
    d_hidden = stud_r * scaled - stud_x * stud_r**3 * inner / DS
    return (d_hidden, d_weight)


def solution(mesh):
    return jax.shard_map(
        per_device,
        mesh=mesh,
        in_specs=(
            P(("pair", "vocab", "tok"), None),
            P(),
            P(None, ("vocab", "tok"), "pair", None),
            P(("vocab", "tok"), "pair"),
            P("pair"),
            P("pair", ("vocab", "tok")),
            P("pair"),
        ),
        out_specs=(P(("vocab", "tok"), "pair"), P("pair", ("vocab", "tok"))),
        check_vma=False,
    )
```

profile of v0, /device:TPU:31, one launch (start us, length us, event | category | flops | bytes accessed | tf_op | source)
XLA Modules:
  0.0 1049.5 jit_solution(16574254247529510625)
XLA Ops:
  7.2 0.0 all-gather.5.cloned.1.call-start
  7.2 0.9 fusion.8
  8.1 3.8 psum.28
  11.9 1.4 fusion.10
  13.3 0.0 all-gather.5.cloned.1.call-update
  13.4 0.0 all-gather.9.cloned.1.call-start
  13.4 0.9 fusion.5
  14.3 1.5 fusion.15
  15.8 0.0 all-gather.9.cloned.1.call-update
  15.8 0.0 reduce-scatter.3.cloned.1.call-start
  15.9 65.1 %all-gather.5.cloned.1.call-done = bf16[512,1792]{1,0:T(8,128)(2,1)} async-done(((bf16[8,1792]{1,0:T(8,128)(2,1)}), bf16[512,1792]{1,0:T(8,128)(2,1)}) %all-gather.5.cloned.1.call-update) | async-done | bytes 1835024 | tf_op jit(solution)/shard_map/all_gather | solution.py:45
  81.0 9.6 fusion.17
  90.6 0.0 all-gather.7.cloned.1.call-start
  90.7 300.5 %all-gather.9.cloned.1.call-done = bf16[128,4,4608]{2,1,0:T(4,128)(2,1)} async-done(((bf16[1,4,4608]{2,1,0:T(4,128)(2,1)}), bf16[128,4,4608]{2,1,0:T(4,128)(2,1)}) %all-gather.9.cloned.1.call-update) | async-done | bytes 4718608 | tf_op jit(solution)/shard_map/all_gather | solution.py:36
  391.2 7.2 reshape.33
  398.4 9.4 fusion.16
  407.8 64.8 %psum.30 = f32[512]{0:T(512)S(1)} all-reduce(f32[512]{0:T(512)S(1)} %get-tuple-element.4), channel_id=1, replica_groups=mesh['pair'=2,'vocab'=8,'tok'=8] {'pair','vocab','tok'}, use_global_device_ids=true, to_apply=%region_7.0 | all-reduce | flops 512 | bytes 4096 | tf_op jit(solution)/shard_map/psum | solution.py:57
  472.6 0.3 divide_convert_fusion
  472.9 14.6 %all_to_all.13 = bf16[2,256,1024]{2,1,0:T(8,128)(2,1)S(1)} all-to-all(bf16[2,256,1024]{2,1,0:T(8,128)(2,1)S(1)} %bitcast.22), channel_id=1, replica_groups=mesh['pair'=2,'vocab'=8,'tok'=8] {'pair'}, dimensions={0} | all-to-all | bytes 2097152 | tf_op jit(solution)/shard_map/all_to_all | solution.py:59
  487.5 0.2 convert_bitcast_fusion
  487.8 1.5 copy.11
  489.2 2.4 fusion.2
  491.6 153.9 %psum.29 = f32[256]{0:T(256)S(1)} all-reduce(f32[256]{0:T(256)S(1)} %fusion.2), channel_id=1, replica_groups=mesh['pair'=2,'vocab'=8,'tok'=8] {'vocab','tok'}, use_global_device_ids=true, to_apply=%region_4.0 | all-reduce | flops 256 | bytes 2048 | tf_op jit(solution)/shard_map/psum | solution.py:60
  645.5 3.4 multiply_convert_fusion
  648.9 0.2 reduce-scatter.5.cloned.1.call-start
  649.1 43.1 %all-gather.7.cloned.1.call-done = bf16[512,2048]{1,0:T(8,128)(2,1)} async-done(((bf16[256,2048]{1,0:T(8,128)(2,1)}), bf16[512,2048]{1,0:T(8,128)(2,1)}) %all-gather.7.cloned.1.call-update) | async-done | bytes 2097168 | tf_op jit(solution)/shard_map/all_gather | solution.py:66
  692.2 9.5 fusion.18
  701.8 328.1 %reduce-scatter.5.cloned.1.call-done = f32[8,1792]{1,0:T(8,128)} async-done(((f32[512,1792]{1,0:T(8,128)}), f32[8,1792]{1,0:T(8,128)}) %reduce-scatter.5.cloned.1.call-update) | async-done | bytes 57360 | tf_op jit(solution)/shard_map/reduce_scatter | solution.py:71
  1029.9 0.9 fusion.14
  1030.8 7.7 convolution_convert_fusion
  1038.5 3.8 psum.31
  1042.3 0.7 fusion.13
  (18 shorter events, 0.1 us)
Async XLA Ops:
  7.2 73.8 %all-gather.5.cloned.1.call-start = ((), (), s32[]{:S(2)}) async-start(), calls=%async_computation.3 | async-start | bytes 1863680 | tf_op jit(solution)/shard_map/all_gather | solution.py:45
  13.4 377.8 %all-gather.9.cloned.1.call-start = ((), (), s32[]{:S(2)}) async-start(), calls=%async_computation.7 | async-start | bytes 4755456 | tf_op jit(solution)/shard_map/all_gather | solution.py:36
  15.8 473.4 %reduce-scatter.3.cloned.1.call-start = ((), (), s32[]{:S(2)}) async-start(), calls=%async_computation.4 | async-start | bytes 6291456 | tf_op jit(solution)/shard_map/reduce_scatter | solution.py:48
  90.6 601.6 %all-gather.7.cloned.1.call-start = ((), (), s32[]{:S(2)}) async-start(), calls=%async_computation.5 | async-start | bytes 3145728 | tf_op jit(solution)/shard_map/all_gather | solution.py:66
  489.2 156.3 %copy-start.4 = (f32[256]{0:T(256)S(1)}, f32[256]{0:T(256)}, u32[]{:S(2)}) copy-start(f32[256]{0:T(256)} %param.13) | copy-start | bytes 3076
  489.2 156.3 %copy-start = (f32[256,2048]{1,0:T(8,128)S(1)}, f32[256,2048]{1,0:T(8,128)}, u32[]{:S(2)}) copy-start(f32[256,2048]{1,0:T(8,128)} %reduce-scatter.3.cloned.1.call-done) | copy-start | bytes 6291460
  648.9 381.0 %reduce-scatter.5.cloned.1.call-start = ((), (), s32[]{:S(2)}) async-start(), calls=%async_computation.6 | async-start | bytes 3727360 | tf_op jit(solution)/shard_map/reduce_scatter | solution.py:71
  701.8 328.1 %copy-start.1 = (bf16[8,1792]{1,0:T(8,128)(2,1)S(1)}, bf16[8,1792]{1,0:T(8,128)(2,1)}, u32[]{:S(2)}) copy-start(bf16[8,1792]{1,0:T(8,128)(2,1)} %param.10) | copy-start | bytes 86020
  701.8 328.1 %copy-start.3 = (f32[1792]{0:T(1024)S(1)}, f32[1792]{0:T(1024)}, u32[]{:S(2)}) copy-start(f32[1792]{0:T(1024)} %param.11) | copy-start | bytes 21508
  701.8 329.0 %copy-start.5 = (bf16[512,1792]{1,0:T(8,128)(2,1)S(1)}, bf16[512,1792]{1,0:T(8,128)(2,1)}, u32[]{:S(2)}) copy-start(bf16[512,1792]{1,0:T(8,128)(2,1)} %all-gather.5.cloned.1.call-done) | copy-start | bytes 5505028
  1030.8 11.5 %copy-start.2 = (f32[8,1792]{1,0:T(8,128)S(1)}, f32[8,1792]{1,0:T(8,128)}, u32[]{:S(2)}) copy-start(f32[8,1792]{1,0:T(8,128)} %reduce-scatter.5.cloned.1.call-done) | copy-start | bytes 172036
Sparse Core Ops, SparseCore 0:
  13.5 67.4 all-gather.4
  83.2 307.8 all-gather.8
  393.6 59.7 reduce-scatter.2
  649.0 43.1 all-gather.6
  701.9 327.8 reduce-scatter.4
where the time goes:
time: 1060 us; the launch traced here: 1050 us
  waiting for transfers between devices  737 us (70%)
  blocking collectives  241 us (23%)
  matrix products  36.3 us (3%)
  between operations  13.8 us (1%)
  other arithmetic  12.7 us (1%)
    reduce_scatter x1, waiting for transfers between devices, per_device(): lax.psum_scatter(lax.dot_general(rows, student_weight, (((1,), (1,)), (()...  328 us
    all_gather x1, waiting for transfers between devices, per_device(): lax.all_gather(normed_t, ('pair', 'vocab', 'tok'), axis=0, tiled=True)  301 us
    psum x1, blocking collectives, per_device(): stud_total = lax.psum(jnp.sum(stud_e, axis=-1), ('vocab', 'tok'))  154 us
    all_gather x1, waiting for transfers between devices, per_device(): gathered_s = lax.all_gather(normed_s, ('vocab', 'tok'), axis=0, tiled=True)  65.1 us
    psum x1, blocking collectives, per_device(): teach_total = lax.psum(jnp.sum(teach_e, axis=-1), ('pair', 'vocab', 'tok'))  64.8 us
    all_gather x1, waiting for transfers between devices, per_device(): grads_all = lax.all_gather(logit_grad, 'pair', axis=0, tiled=True)  43.1 us
  transfers between devices with their start and end apart: 5, of which 4 were waited for; matrix products, arithmetic and copies ran while one was open for 3% of the time, Pallas kernels for 0%

commit v1 on v0

v1 whole, which is shorter than its diff:
```python
import jax
import jax.numpy as jnp
from jax import lax
from jax.experimental import pallas as pl
from jax.experimental.pallas import tpu as pltpu
from jax.sharding import PartitionSpec as P

DT = 4608
DS = 3584
HS = DS // 2
CS = HS // 2
VT = 1024
EPS = 1e-06
CAP = 30.0
KT = DT // 4
MESH = pl.DeviceIdType.MESH

SLOPE = 3.0
KNEE = 64.0
LOGK = 7.2
BIAS = 125.0
LOG2E = 1.4426950408889634


def encode(b):
    a = jnp.abs(b)
    far = SLOPE * KNEE + LOGK * LOG2E * jnp.log(jnp.maximum(a, KNEE) / KNEE)
    w = jnp.where(a <= KNEE, SLOPE * a, jnp.minimum(far, 251.5)) - BIAS
    y = jnp.exp2(w)
    return jnp.where(b < 0, -y, y).astype(jnp.bfloat16)


def decode(code):
    y = code.astype(jnp.float32)
    w = jnp.log(jnp.abs(y)) * LOG2E + BIAS
    a = jnp.where(
        w <= SLOPE * KNEE,
        jnp.maximum(w, 0.0) * (1.0 / SLOPE),
        KNEE * jnp.exp2((w - SLOPE * KNEE) * (1.0 / LOGK)),
    )
    return jnp.where(y < 0, -a, a)


def row_sums(e):
    part = e[:, :128]
    for n in range(1, e.shape[1] // 128):
        part = part + e[:, n * 128 : (n + 1) * 128]
    return jnp.sum(part.T, axis=0, keepdims=True)


def column(row):
    return jnp.broadcast_to(row, (128, 128)).T


def head_kernel(
    th, tg, sh, sg, tw, wt_hbm, ws_hbm,
    dh_out, s_out, g_out,
    wt, ws, tsc, tb, tn, sq, nf, stile, s_all, zs, zr, zo, slope, et, g_all, tw2,
    ar_s, ar_r, ar2, ar3, dacc, rsib_s, rsib_r, rs_s, rs_r, fin_s, fin, inn,
    ssem, rsem, lsem,
):
    p = lax.axis_index("pair")
    v = lax.axis_index("vocab")
    t = lax.axis_index("tok")
    x, c, h, z = v // 2, lax.rem(v, 2), t // 4, lax.rem(t, 4)
    y = 2 * h + p

    def dev(p_, x_, c_, h_, z_):
        return (p_, 2 * x_ + c_, 4 * h_ + z_)

    partner = dev(1 - p, x, c, h, z)
    sibling = dev(p, x, 1 - c, h, z)

    def xdev(d):
        return dev(p, lax.rem(x + d, 4), c, h, z)

    def zdev(d):
        return dev(p, x, c, h, lax.rem(z + d, 4))

    def ydev(d):
        y_ = lax.rem(y + d, 4)
        return dev(lax.rem(y_, 2), x, c, y_ // 2, z)

    def plane_dev(k):
        return lax.rem(x + k, 4), lax.rem(z + k // 4, 4), lax.rem(h + k // 16, 2)

    def flat_dev(k):
        x_, z_, h_ = plane_dev(k)
        return dev(p, x_, c, h_, z_)

    counter = [0]
    sends = []

    def rcopy(src, dst, device):
        i = counter[0]
        counter[0] += 1
        cp = pltpu.make_async_remote_copy(
            src_ref=src, dst_ref=dst, send_sem=ssem.at[i], recv_sem=rsem.at[i],
            device_id=device, device_id_type=MESH,
        )
        cp.start()
        sends.append(cp)
        return cp

    def rwait(region, sem):
        pltpu.make_async_remote_copy(
            src_ref=region, dst_ref=region, send_sem=sem, recv_sem=sem,
            device_id=partner, device_id_type=MESH,
        ).wait_recv()

    w_cp = [
        pltpu.make_async_copy(ws_hbm.at[:, pl.ds(pl.multiple_of((1 - p) * VT, VT), VT)], ws.at[1], lsem.at[0]),
        pltpu.make_async_copy(ws_hbm.at[:, pl.ds(pl.multiple_of(p * VT, VT), VT)], ws.at[0], lsem.at[1]),
        pltpu.make_async_copy(wt_hbm, wt, lsem.at[2]),
    ]
    for cp in w_cp:
        cp.start()

    bar = pltpu.get_barrier_semaphore()
    for d in (sibling, partner, ydev(3 - 2 * p)):
        pl.semaphore_signal(bar, inc=1, device_id=d, device_id_type=MESH)

    @pl.loop(1, 32)
    def _(k):
        pl.semaphore_signal(bar, inc=1, device_id=flat_dev(k), device_id_type=MESH)

    sx = sh[...].astype(jnp.float32)
    sq[0] = jnp.broadcast_to(jnp.sum(sx * sx, axis=-1, keepdims=True), (8, 128))
    tx = th[...].astype(jnp.float32)
    tnorm = tx * lax.rsqrt(jnp.mean(tx * tx, axis=-1, keepdims=True) + EPS) * tg[...]
    for j in range(4):
        tsc[4 * j : 4 * j + 4, :] = tnorm[:, j * KT : (j + 1) * KT]
    tb[c, y, x, z] = tsc[...].astype(jnp.bfloat16)
    tw2[p] = tw[...]

    pl.semaphore_wait(bar, 34)

    sq_cp = rcopy(sq.at[0], sq.at[1], partner)
    tw_cp = rcopy(tw2.at[p], tw2.at[p], partner)
    own_t = tb.at[c, y, x, z]
    t1 = [rcopy(own_t, own_t, ydev(d)) for d in (1, 2, 3)]

    sq_cp.wait_recv()
    stud_r = lax.rsqrt((sq[0] + sq[1])[:, :1] / DS + EPS)
    snorm = sx * stud_r * sg[...]
    nf[0] = snorm[:, :CS]
    nf[1] = snorm[:, CS:]
    mine = stile.at[pl.ds(pl.multiple_of(c * 8, 8), 8)]
    n_cp = rcopy(nf.at[1 - c], mine, sibling)
    mine[...] = nf[c]
    n_cp.wait_recv()
    ccol = pl.ds(pl.multiple_of(c * CS, 128), CS)
    srows = pl.ds(pl.multiple_of(h * 256 + x * 64 + z * 16, 16), 16)
    s_all[srows, ccol] = stile[...].astype(jnp.bfloat16)
    own_s = s_all.at[srows, ccol]
    s_sem = counter[0]
    counter[0] += 2

    def s_send(k):
        return pltpu.make_async_remote_copy(
            src_ref=own_s, dst_ref=own_s, send_sem=ssem.at[s_sem], recv_sem=rsem.at[s_sem + h],
            device_id=flat_dev(k), device_id_type=MESH,
        )

    @pl.loop(1, 32)
    def _(k):
        s_send(k).start()

    for cp in t1:
        cp.wait_recv()
    t2 = [rcopy(tb.at[c, pl.ds(0, 2), x, z], tb.at[c, pl.ds(0, 2), x, z], xdev(d)) for d in (1, 2, 3)]
    t2 += [rcopy(tb.at[c, pl.ds(2, 2), x, z], tb.at[c, pl.ds(2, 2), x, z], zdev(d)) for d in (1, 2, 3)]
    for cp in w_cp:
        cp.wait()

    sib_s = []
    for k in range(2):
        @pl.when(h == k)
        def _():
            rwait(s_all.at[pl.ds(k * 256, 240), ccol], rsem.at[s_sem + k])

        @pl.when(h != k)
        def _():
            rwait(s_all.at[pl.ds(k * 256, 256), ccol], rsem.at[s_sem + k])

        region = s_all.at[pl.ds(k * 256, 256), ccol]
        sib_s.append(rcopy(region, region, sibling))
        if k == 0:
            for cp in t2:
                cp.wait_recv()
            t3 = []
            for d in (1, 2, 3):
                a = tb.at[c, pl.ds(0, 2), :, z]
                t3.append(rcopy(a, a, zdev(d)))
                b = tb.at[c, pl.ds(2, 2), x]
                t3.append(rcopy(b, b, xdev(d)))
            sib_t = []
            for r in (tb.at[c, pl.ds(0, 2), :, z], tb.at[c, pl.ds(2, 2), x]):
                sib_t.append(rcopy(r, r, sibling))

    z_cp = []
    for k in range(2):
        sib_s[k].wait_recv()
        rows = pl.ds(k * 256, 256)

        @pl.loop(0, 4)
        def _(n):
            cols = pl.ds(pl.multiple_of(n * 256, 256), 256)
            zs[rows, cols] = encode(jnp.dot(s_all[rows, :], ws[1, :, cols], preferred_element_type=jnp.float32))

        z_cp.append(rcopy(zs.at[rows], zr.at[rows], partner))
    s_cp = pltpu.make_async_copy(s_all, s_out, lsem.at[3])
    s_cp.start()

    @pl.loop(0, 4)
    def _(n):
        cols = pl.ds(pl.multiple_of(n * 256, 256), 256)
        zo[:, cols] = jnp.dot(s_all[...], ws[0, :, cols], preferred_element_type=jnp.float32)

    for i, d in enumerate((1, 2, 3)):
        z_, x_ = lax.rem(z - d + 4, 4), lax.rem(x - d + 4, 4)
        t3[2 * i].wait_recv()
        r = tb.at[c, pl.ds(0, 2), :, z_]
        sib_t.append(rcopy(r, r, sibling))
        t3[2 * i + 1].wait_recv()
        r = tb.at[c, pl.ds(2, 2), x_]
        sib_t.append(rcopy(r, r, sibling))
    for cp in sib_t:
        cp.wait_recv()

    o = lax.broadcasted_iota(jnp.int32, (256, 256), 0)
    src = lax.broadcasted_iota(jnp.int32, (256, 256), 1)
    o_j, o_r = o // 64, lax.rem(o, 4)
    o_h, o_z = lax.rem(o // 32, 2), lax.rem(o // 16, 2) * 2 + lax.rem(o // 4, 2)
    o_x = lax.rem(o // 8, 2)
    perm = (src == o_h * 128 + o_x * 64 + o_z * 16 + o_j * 4 + o_r).astype(jnp.bfloat16)

    @pl.loop(0, 8)
    def _(g):
        c_, p_, x_ = g // 4, lax.rem(g // 2, 2), lax.rem(g, 2)
        pieces = [tb[c_, 2 * a + p_, 2 * x_ + b].reshape(64, KT) for a in range(2) for b in range(2)]
        out = jnp.dot(perm, jnp.concatenate(pieces, axis=0), preferred_element_type=jnp.float32)
        out = out.astype(jnp.bfloat16)
        for j in range(4):
            tn[pl.ds(pl.multiple_of(g * 64, 64), 64), j * KT : (j + 1) * KT] = out[j * 64 : (j + 1) * 64]

    @pl.loop(0, 4)
    def _(n):
        cols = pl.ds(pl.multiple_of(n * 256, 256), 256)
        logits = jnp.dot(tn[...], wt[:, cols], preferred_element_type=jnp.float32)
        et[:, cols] = jnp.exp(CAP * jnp.tanh(logits / CAP))

    tw_cp.wait_recv()
    ar_sem = counter[0]
    counter[0] += 2
    slot = h * 16 + x * 4 + z

    def ar_send(k, i):
        return pltpu.make_async_remote_copy(
            src_ref=ar_s.at[k], dst_ref=ar_r.at[k, slot], send_sem=ssem.at[ar_sem + k], recv_sem=rsem.at[ar_sem + k],
            device_id=flat_dev(i), device_id_type=MESH,
        )

    g_cp = []
    gcol = pl.ds(pl.multiple_of(p * VT, VT), VT)
    ocol = pl.ds(pl.multiple_of((1 - p) * VT, VT), VT)
    for k in range(2):
        z_cp[k].wait_recv()
        for i in range(2):
            rows = pl.ds(k * 256 + i * 128, 128)

            @pl.loop(0, 8)
            def _(n):
                cols = pl.ds(pl.multiple_of(n * 128, 128), 128)
                th_ = jnp.tanh((zo[rows, cols] + decode(zr[rows, cols])) / CAP)
                zo[rows, cols] = jnp.exp(CAP * th_)
                slope[rows, cols] = 1.0 - th_ * th_

            ar_s[k, i : i + 1, :] = row_sums(zo[rows, :])
            ar_s[k, 2 + i : 3 + i, :] = row_sums(et[rows, :])
        ar_s[k, 4:8, :] = jnp.zeros((4, 128), jnp.float32)

        @pl.loop(1, 32)
        def _(i):
            ar_send(k, i).start()

        rwait(ar_r.at[k, pl.ds(0, 31)], rsem.at[ar_sem + k])
        ar_r[k, slot] = ar_s[k]
        ar2[k, 0] = jnp.sum(ar_r[k], axis=0)
        rcopy(ar2.at[k, 0], ar2.at[k, 1], sibling).wait_recv()
        ar3[k, 0] = ar2[k, 0] + ar2[k, 1]
        rcopy(ar3.at[k, 0], ar3.at[k, 1], partner).wait_recv()
        total = ar3[k, 0] + ar3[k, 1]
        for i in range(2):
            rows = pl.ds(k * 256 + i * 128, 128)
            w_col = column(tw2[i, k : k + 1, :])
            s_col = 1.0 / column(total[i : i + 1, :])
            t_col = 1.0 / column(total[2 + i : 3 + i, :])

            @pl.loop(0, 8)
            def _(n):
                cols = pl.ds(pl.multiple_of(n * 128, 128), 128)
                probs = (et[rows, cols] * t_col).astype(jnp.bfloat16).astype(jnp.float32)
                grad = w_col * (zo[rows, cols] * s_col - probs) * slope[rows, cols]
                g_all[rows, pl.ds(pl.multiple_of(p * VT + n * 128, 128), 128)] = grad.astype(jnp.bfloat16)

        region = g_all.at[pl.ds(k * 256, 256), gcol]
        g_cp.append(rcopy(region, region, partner))

    nt = (((1,), (1,)), ((), ()))

    @pl.loop(0, 7)
    def _(n):
        w_rows = pl.ds(pl.multiple_of(n * 256, 256), 256)
        dacc[:, w_rows] = lax.dot_general(g_all[:, gcol], ws[0, w_rows, :], nt, preferred_element_type=jnp.float32)

    rs_sem = counter[0]
    counter[0] += 3

    def rs_send(k, i):
        x_, z_ = lax.rem(x + i, 4), lax.rem(z + i // 4, 4)
        return pltpu.make_async_remote_copy(
            src_ref=rs_s.at[k, x_, z_], dst_ref=rs_r.at[slot], send_sem=ssem.at[rs_sem + k], recv_sem=rsem.at[rs_sem + 2],
            device_id=dev(p, x_, c, k, z_), device_id_type=MESH,
        )

    xcol = pl.ds(pl.multiple_of((1 - c) * CS, 128), CS)
    for k in range(2):
        rows = pl.ds(k * 256, 256)
        g_cp[k].wait_recv()

        @pl.loop(0, 7)
        def _(n):
            w_rows = pl.ds(pl.multiple_of(n * 256, 256), 256)
            dacc[rows, w_rows] += lax.dot_general(
                g_all[rows, ocol], ws[1, w_rows, :], nt, preferred_element_type=jnp.float32
            )

        rsib_s[rows, :] = dacc[rows, xcol].astype(jnp.bfloat16)
        rcopy(rsib_s.at[rows], rsib_r.at[rows], sibling).wait_recv()
        both = (dacc[rows, ccol] + rsib_r[rows, :].astype(jnp.float32)).astype(jnp.bfloat16)
        rs_s[k] = both.reshape(4, 4, 16, CS)
        first = jnp.where(h == k, 1, 0)

        @pl.loop(first, 16)
        def _(i):
            rs_send(k, i).start()

    g_out_cp = pltpu.make_async_copy(g_all, g_out, lsem.at[4])
    g_out_cp.start()

    rwait(rs_r.at[pl.ds(0, 31)], rsem.at[rs_sem + 2])
    rs_r[slot] = rs_s[h, x, z]
    done = jnp.sum(rs_r[...].astype(jnp.float32), axis=0)
    fin_s[...] = done
    fin[c] = fin_s[pl.ds(pl.multiple_of(c * 8, 8), 8)]
    rcopy(fin_s.at[pl.ds(pl.multiple_of((1 - c) * 8, 8), 8)], fin.at[c], sibling).wait_recv()
    scaled = jnp.concatenate([fin[0], fin[1]], axis=-1) * sg[...]
    inn[0] = jnp.broadcast_to(jnp.sum(sx * scaled, axis=-1, keepdims=True), (8, 128))
    rcopy(inn.at[0], inn.at[1], partner).wait_recv()
    inner = (inn[0] + inn[1])[:, :1]
    dh_out[...] = stud_r * scaled - sx * (stud_r * stud_r * stud_r) * inner / DS

    for cp in sends:
        cp.wait_send()

    @pl.loop(1, 32)
    def _(k):
        s_send(k).wait_send()
        ar_send(0, k).wait_send()
        ar_send(1, k).wait_send()

    for k in range(2):
        first = jnp.where(h == k, 1, 0)

        @pl.loop(first, 16)
        def _(i):
            rs_send(k, i).wait_send()

    s_cp.wait()
    g_out_cp.wait()


def head(th, tg, sh, sg, tw, wt, ws):
    f32, bf16 = jnp.float32, jnp.bfloat16
    vmem = pl.BlockSpec(memory_space=pltpu.VMEM)
    hbm = pl.BlockSpec(memory_space=pl.ANY)
    scratch = [
        pltpu.VMEM((DT, VT), bf16),
        pltpu.VMEM((2, HS, VT), bf16),
        pltpu.VMEM((16, KT), f32),
        pltpu.VMEM((2, 4, 4, 4, 16, KT), bf16),
        pltpu.VMEM((512, DT), bf16),
        pltpu.VMEM((2, 8, 128), f32),
        pltpu.VMEM((2, 8, CS), f32),
        pltpu.VMEM((16, CS), f32),
        pltpu.VMEM((512, HS), bf16),
        pltpu.VMEM((512, VT), bf16),
        pltpu.VMEM((512, VT), bf16),
        pltpu.VMEM((512, VT), f32),
        pltpu.VMEM((512, VT), f32),
        pltpu.VMEM((512, VT), f32),
        pltpu.VMEM((512, 2 * VT), bf16),
        pltpu.VMEM((2, 8, 128), f32),
        pltpu.VMEM((2, 8, 128), f32),
        pltpu.VMEM((2, 32, 8, 128), f32),
        pltpu.VMEM((2, 2, 8, 128), f32),
        pltpu.VMEM((2, 2, 8, 128), f32),
        pltpu.VMEM((512, HS), f32),
        pltpu.VMEM((512, CS), bf16),
        pltpu.VMEM((512, CS), bf16),
        pltpu.VMEM((2, 4, 4, 16, CS), bf16),
        pltpu.VMEM((32, 16, CS), bf16),
        pltpu.VMEM((16, CS), f32),
        pltpu.VMEM((2, 8, CS), f32),
        pltpu.VMEM((2, 8, 128), f32),
        pltpu.SemaphoreType.DMA((64,)),
        pltpu.SemaphoreType.DMA((64,)),
        pltpu.SemaphoreType.DMA((5,)),
    ]
    return pl.pallas_call(
        head_kernel,
        out_shape=(
            jax.ShapeDtypeStruct((8, HS), f32),
            jax.ShapeDtypeStruct((512, HS), bf16),
            jax.ShapeDtypeStruct((512, 2 * VT), bf16),
        ),
        in_specs=[vmem] * 5 + [hbm] * 2,
        out_specs=(vmem, hbm, hbm),
        scratch_shapes=scratch,
        compiler_params=pltpu.CompilerParams(
            collective_id=0, has_side_effects=True, vmem_limit_bytes=58 * 1024 * 1024
        ),
        name="head",
    )(th, tg, sh, sg, tw, wt, ws)


def per_device(
    teacher_hidden,
    teacher_gain,
    teacher_weight,
    student_hidden,
    student_gain,
    student_weight,
    token_weight,
):
    tw = token_weight.reshape(2, 2, 2, 4, 8).transpose(2, 0, 3, 1, 4).reshape(2, 128)
    tw = jnp.pad(tw, ((0, 6), (0, 0)))
    d_hidden, s_all, g_all = head(
        teacher_hidden,
        teacher_gain.reshape(1, DT),
        student_hidden,
        student_gain.reshape(1, HS),
        tw,
        teacher_weight.reshape(DT, VT),
        student_weight,
    )
    d_weight = lax.dot_general(
        s_all, g_all, (((0,), (0,)), ((), ())), preferred_element_type=jnp.float32
    ).astype(jnp.bfloat16)
    return (d_hidden, d_weight)


def solution(mesh):
    return jax.shard_map(
        per_device,
        mesh=mesh,
        in_specs=(
            P(("pair", "vocab", "tok"), None),
            P(),
            P(None, ("vocab", "tok"), "pair", None),
            P(("vocab", "tok"), "pair"),
            P("pair"),
            P("pair", ("vocab", "tok")),
            P("pair"),
        ),
        out_specs=(P(("vocab", "tok"), "pair"), P("pair", ("vocab", "tok"))),
        check_vma=False,
    )
```

time: 1060 us -> 142 us (0.13)
  waiting for transfers between devices: 737 us -> 0 us
  blocking collectives: 241 us -> 0 us
  Pallas kernels: 0 us -> 126 us
  matrix products: 36.3 us -> 9.22 us
  between operations: 13.8 us -> 0.66 us
  other arithmetic: 12.7 us -> 0 us
    all_gather x3 -> x0, waiting for transfers between devices: 409 us -> none  [the longest x1 301 us: per_device(): lax.all_gather(normed_t, ('pair', 'vocab', 'tok'), axis=0, tiled=True)]
    reduce_scatter x2 -> x0, waiting for transfers between devices: 328 us -> none  [the longest x1 328 us: per_device(): lax.psum_scatter(lax.dot_general(rows, student_weight, (((1,), (1,)), (()...]
    psum x4 -> x0, blocking collectives: 226 us -> none  [the longest x1 154 us: per_device(): stud_total = lax.psum(jnp.sum(stud_e, axis=-1), ('vocab', 'tok'))]
    pallas_call x0 -> x1, Pallas kernels: none -> 126 us  [head(): pl.pallas_call(head_kernel, out_shape=(jax.ShapeDtypeStruct((8, HS), f32)...]
    dot_general x4 -> x1, matrix products: 36.3 us -> 9.22 us  [per_device(): lax.dot_general(s_all, g_all, (((0,), (0,)), ((), ())), preferred_element...]
    all_to_all x1 -> x0, blocking collectives: 14.6 us -> none  [per_device(): lax.all_to_all(probs_t, 'pair', split_axis=0, concat_axis=1, tiled=True)]
  transfers between devices with their start and end apart: 5 -> 0, of which waited for: 4 -> 0; matrix products, arithmetic and copies ran while one was open for 3% -> 0% of each run, Pallas kernels for 0% -> 0%
where the time goes in v1:
time: 142 us; the launch traced here: 140 us
  Pallas kernels  126 us (89%)
  matrix products  9.22 us (6%)
  local copies, waits for them, and re-layouts  4.75 us (3%)
    pallas_call x1, Pallas kernels, head(): pl.pallas_call(head_kernel, out_shape=(jax.ShapeDtypeStruct((8, HS), f32)...  126 us
    dot_general x1, matrix products, per_device(): lax.dot_general(s_all, g_all, (((0,), (0,)), ((), ())), preferred_element...  9.22 us

profile of v1, /device:TPU:31, one launch (start us, length us, event | category | flops | bytes accessed | tf_op | source)
XLA Modules:
  0.0 140.2 jit_solution(6991904553646862171)
XLA Ops:
  0.6 1.3 reshape.20.sg
  1.9 0.8 reshape.21
  2.7 0.1 reshape.22
  2.8 0.6 pad.4.tw
  3.4 1.3 reshape.19.tg
  4.8 125.5 %head.1 = (f32[8,1792]{1,0:T(8,128)}, bf16[512,1792]{1,0:T(8,128)(2,1)}, bf16[512,2048]{1,0:T(8,128)(2,1)}) custom-call(bf16[4,4608]{1,0:T(4,128)(2,1)} %th.1, f32[1,4608]{1,0:T(1,128)} %reshape.19.tg, bf16[8,1792]{1,0:T(8,128)(2,1)} %sh.1, f32[1,1792]{1,0:T(1,128)} %reshape.20.sg, f32[8,128]{1,0:T(8,128)} %pad.4.tw, bf16[4608,1024]{1,0:T(8,128)(2,1)} %bitcast.4, ...), custom_call_target="tpu_custom_call" | custom-call | tf_op jit(solution)/shard_map/head/pallas_call | solution.py:421
  130.3 0.0 copy-start
  130.3 9.2 %convolution_convert_fusion = bf16[1792,2048]{1,0:T(8,128)(2,1)} fusion(bf16[512,1792]{1,0:T(8,128)(2,1)} %get-tuple-element.6, bf16[512,2048]{1,0:T(8,128)(2,1)} %get-tuple-element.7), kind=kOutput, calls=%fused_computation | convolution fusion | flops 3761766400 | bytes 11272192 | tf_op jit(solution)/shard_map/dot_general | solution.py:458
  139.5 0.0 copy-done
  139.5 0.6 copy.11
  (1 shorter events, 0.0 us)
Async XLA Ops:
  130.3 9.2 %copy-start = (f32[8,1792]{1,0:T(8,128)S(1)}, f32[8,1792]{1,0:T(8,128)}, u32[]{:S(2)}) copy-start(f32[8,1792]{1,0:T(8,128)} %get-tuple-element.10) | copy-start | bytes 172036

commit v2 on v1

v2 whole, which is shorter than its diff:
```python
import jax
import jax.numpy as jnp
from jax import lax
from jax.experimental import pallas as pl
from jax.experimental.pallas import tpu as pltpu
from jax.sharding import PartitionSpec as P

DT = 4608
DS = 3584
HS = DS // 2
CS = HS // 2
VT = 1024
EPS = 1e-06
CAP = 30.0
KT = DT // 4
MESH = pl.DeviceIdType.MESH

SLOPE = 3.0
KNEE = 64.0
LOGK = 7.2
BIAS = 125.0
LOG2E = 1.4426950408889634


def encode(b):
    a = jnp.abs(b)
    far = SLOPE * KNEE + LOGK * LOG2E * jnp.log(jnp.maximum(a, KNEE) / KNEE)
    w = jnp.where(a <= KNEE, SLOPE * a, jnp.minimum(far, 251.5)) - BIAS
    y = jnp.exp2(w)
    return jnp.where(b < 0, -y, y).astype(jnp.bfloat16)


def decode(code):
    y = code.astype(jnp.float32)
    w = jnp.log(jnp.abs(y)) * LOG2E + BIAS
    a = jnp.where(
        w <= SLOPE * KNEE,
        jnp.maximum(w, 0.0) * (1.0 / SLOPE),
        KNEE * jnp.exp2((w - SLOPE * KNEE) * (1.0 / LOGK)),
    )
    return jnp.where(y < 0, -a, a)


def row_sums(e):
    part = e[:, :128]
    for n in range(1, e.shape[1] // 128):
        part = part + e[:, n * 128 : (n + 1) * 128]
    return jnp.sum(part.T, axis=0, keepdims=True)


def column(row):
    return jnp.broadcast_to(row, (128, 128)).T


def head_kernel(
    th, tg, sh, sg, tw, wt_hbm, ws_hbm,
    dh_out, s_out, g_out,
    wt, ws, tsc, tb, tn, sq, nf, stile, s_all, st, zs, zr, zo, slope, et, g_all, tw2,
    ar_s, ar_c, ar_r, ar_y, dacc, rsib_s, rsib_r, rs_s, rs_r, fin_s, fin, inn,
    ssem, rsem, lsem,
):
    p = lax.axis_index("pair")
    v = lax.axis_index("vocab")
    t = lax.axis_index("tok")
    x, c, h, z = v // 2, lax.rem(v, 2), t // 4, lax.rem(t, 4)
    y = 2 * h + p

    def dev(p_, x_, c_, h_, z_):
        return (p_, 2 * x_ + c_, 4 * h_ + z_)

    partner = dev(1 - p, x, c, h, z)
    sibling = dev(p, x, 1 - c, h, z)
    xs = [x] + [lax.rem(x + d, 4) for d in (1, 2, 3)]
    zs_ = [z] + [lax.rem(z + d, 4) for d in (1, 2, 3)]
    xdev = [dev(p, xs[d], c, h, z) for d in range(4)]
    zdev = [dev(p, x, c, h, zs_[d]) for d in range(4)]
    ys = [y] + [lax.rem(y + d, 4) for d in (1, 2, 3)]
    ydev = [dev(lax.rem(ys[d], 2), x, c, ys[d] // 2, z) for d in range(4)]
    hdev = ydev[2]
    cross = dev(p, x, 1 - c, 1 - h, z)
    plane = [(a, b) for b in range(4) for a in range(4)]

    counter = [0]
    sends = []
    ends = []

    class Copy:
        def __init__(self, i, src, dst, device):
            self.cp = pltpu.make_async_remote_copy(
                src_ref=src, dst_ref=dst, send_sem=ssem.at[i], recv_sem=rsem.at[i],
                device_id=device, device_id_type=MESH,
            )
            self.cp.start()
            self.here = False

        def wait_recv(self):
            if not self.here:
                self.cp.wait_recv()
            self.here = True

    def rcopy(src, dst, device):
        i = counter[0]
        counter[0] += 1
        sends.append(Copy(i, src, dst, device))
        return sends[-1]

    def finish():
        for cp in sends:
            cp.wait_recv()
            cp.cp.wait_send()
        for end in ends:
            end()

    def rwait(region, sem):
        pltpu.make_async_remote_copy(
            src_ref=region, dst_ref=region, send_sem=sem, recv_sem=sem,
            device_id=partner, device_id_type=MESH,
        ).wait_recv()

    w_cp = [
        pltpu.make_async_copy(ws_hbm.at[:, pl.ds(pl.multiple_of((1 - p) * VT, VT), VT)], ws.at[1], lsem.at[0]),
        pltpu.make_async_copy(ws_hbm.at[:, pl.ds(pl.multiple_of(p * VT, VT), VT)], ws.at[0], lsem.at[1]),
        pltpu.make_async_copy(wt_hbm, wt, lsem.at[2]),
    ]
    for cp in w_cp:
        cp.start()
    w_here = []

    def w_wait():
        if not w_here:
            for cp in w_cp:
                cp.wait()
        w_here.append(True)

    ends.append(w_wait)

    bar = pltpu.get_barrier_semaphore()
    for d in [sibling, ydev[1], ydev[2], ydev[3], cross]:
        pl.semaphore_signal(bar, inc=1, device_id=d, device_id_type=MESH)
    for a, b in plane[1:]:
        pl.semaphore_signal(bar, inc=1, device_id=dev(p, xs[a], c, h, zs_[b]), device_id_type=MESH)

    sx = sh[...].astype(jnp.float32)
    sq[0] = jnp.broadcast_to(jnp.sum(sx * sx, axis=-1, keepdims=True), (8, 128))
    tx = th[...].astype(jnp.float32)
    tnorm = tx * lax.rsqrt(jnp.mean(tx * tx, axis=-1, keepdims=True) + EPS) * tg[...].reshape(1, DT)
    for j in range(4):
        tsc[4 * j : 4 * j + 4, :] = tnorm[:, j * KT : (j + 1) * KT]
    tb[c, y, x, z] = tsc[...].astype(jnp.bfloat16)
    for b in range(2):
        tw2[p, b] = jnp.broadcast_to(tw[pl.ds(128 * b, 128)].reshape(1, 128), (8, 128))

    pl.semaphore_wait(bar, 20)

    sq_cp = rcopy(sq.at[0], sq.at[1], partner)
    tw_cp = rcopy(tw2.at[p], tw2.at[p], partner)
    own_t = tb.at[c, y, x, z]
    t1 = [rcopy(own_t, own_t, ydev[d]) for d in (1, 2, 3)]

    sq_cp.wait_recv()
    stud_r = lax.rsqrt((sq[0] + sq[1])[:, :1] / DS + EPS)
    gain = sg[...].reshape(1, HS)
    snorm = sx * stud_r * gain
    nf[0] = snorm[:, :CS]
    nf[1] = snorm[:, CS:]
    mine = stile.at[pl.ds(pl.multiple_of(c * 8, 8), 8)]
    n_cp = rcopy(nf.at[1 - c], mine, sibling)
    mine[...] = nf[c]
    n_cp.wait_recv()
    ccol = pl.ds(pl.multiple_of(c * CS, 128), CS)
    s_all[h, x, z, :, ccol] = stile[...].astype(jnp.bfloat16)
    own_s = s_all.at[h, x, z, :, ccol]
    h_cp = rcopy(own_s, own_s, hdev)
    h_cp.wait_recv()
    s2 = []
    for d in (1, 2, 3):
        a, b = s_all.at[0, x, z, :, ccol], s_all.at[1, x, z, :, ccol]
        s2.append(rcopy(a, a, xdev[d]))
        s2.append(rcopy(b, b, zdev[d]))
    for cp in t1:
        cp.wait_recv()
    t2 = []
    for d in (1, 2, 3):
        a, b = tb.at[c, pl.ds(0, 2), x, z], tb.at[c, pl.ds(2, 2), x, z]
        t2.append(rcopy(a, a, xdev[d]))
        t2.append(rcopy(b, b, zdev[d]))
    for cp in s2:
        cp.wait_recv()
    s3 = []
    for d in (1, 2, 3):
        a, b = s_all.at[0, :, z, :, ccol], s_all.at[1, x, :, :, ccol]
        s3.append(rcopy(a, a, zdev[d]))
        s3.append(rcopy(b, b, xdev[d]))
    for cp in t2:
        cp.wait_recv()
    t3 = []
    for d in (1, 2, 3):
        a, b = tb.at[c, pl.ds(0, 2), :, z], tb.at[c, pl.ds(2, 2), x]
        t3.append(rcopy(a, a, zdev[d]))
        t3.append(rcopy(b, b, xdev[d]))
    sib_t = []
    for r in (tb.at[c, pl.ds(0, 2), :, z], tb.at[c, pl.ds(2, 2), x]):
        sib_t.append(rcopy(r, r, sibling))
    sib_s = ([], [])
    for i in range(4):
        if i:
            s3[2 * i - 2].wait_recv()
        r = s_all.at[0, :, zs_[(4 - i) % 4], :, ccol]
        sib_s[0].append(rcopy(r, r, sibling))
    for i in range(4):
        if i:
            s3[2 * i - 1].wait_recv()
        r = s_all.at[1, xs[(4 - i) % 4], :, :, ccol]
        sib_s[1].append(rcopy(r, r, sibling))
    w_wait()

    z_cp = ([], [])
    for k in range(2):
        for cp in sib_s[k]:
            cp.wait_recv()
        rows = pl.ds(k * 256, 256)
        lhs = s_all[k].reshape(256, HS)
        for n in range(4):
            cols = pl.ds(n * 256, 256)
            zs[rows, cols] = encode(jnp.dot(lhs, ws[1, :, cols], preferred_element_type=jnp.float32))
            z_cp[k].append(rcopy(zs.at[rows, cols], zr.at[rows, cols], partner))


    def own_logits(k):
        rows = pl.ds(k * 256, 256)

        @pl.loop(0, 4)
        def _(n):
            cols = pl.ds(pl.multiple_of(n * 256, 256), 256)
            zo[rows, cols] = jnp.dot(s_all[k].reshape(256, HS), ws[0, :, cols], preferred_element_type=jnp.float32)

    own_logits(0)
    own_logits(1)
    for k in range(2):
        for j in range(7):
            cols = pl.ds(j * 256, 256)
            st[j * 256 : (j + 1) * 256, k * 256 : (k + 1) * 256] = s_all[k, :, :, :, cols].reshape(256, 256).T
    s_cp = pltpu.make_async_copy(st, s_out, lsem.at[3])
    s_cp.start()
    ends.append(s_cp.wait)
    for i, d in enumerate((1, 2, 3)):
        z_, x_ = zs_[4 - d], xs[4 - d]
        t3[2 * i].wait_recv()
        r = tb.at[c, pl.ds(0, 2), :, z_]
        sib_t.append(rcopy(r, r, sibling))
        t3[2 * i + 1].wait_recv()
        r = tb.at[c, pl.ds(2, 2), x_]
        sib_t.append(rcopy(r, r, sibling))
    for cp in sib_t:
        cp.wait_recv()

    o = lax.broadcasted_iota(jnp.int32, (256, 256), 0)
    src = lax.broadcasted_iota(jnp.int32, (256, 256), 1)
    o_j, o_r = o // 64, lax.rem(o, 4)
    o_h, o_z = lax.rem(o // 32, 2), lax.rem(o // 16, 2) * 2 + lax.rem(o // 4, 2)
    o_x = lax.rem(o // 8, 2)
    perm = (src == o_h * 128 + o_x * 64 + o_z * 16 + o_j * 4 + o_r).astype(jnp.bfloat16)

    def teacher(k):
        @pl.loop(4 * k, 4 * k + 4)
        def _(g):
            c_, p_, x_ = g // 4, lax.rem(g // 2, 2), lax.rem(g, 2)
            pieces = [tb[c_, 2 * a + p_, 2 * x_ + b].reshape(64, KT) for a in range(2) for b in range(2)]
            out = jnp.dot(perm, jnp.concatenate(pieces, axis=0), preferred_element_type=jnp.float32)
            out = out.astype(jnp.bfloat16)
            for j in range(4):
                tn[pl.ds(pl.multiple_of(g * 64, 64), 64), j * KT : (j + 1) * KT] = out[j * 64 : (j + 1) * 64]

        rows = pl.ds(k * 256, 256)

        @pl.loop(0, 4)
        def _(n):
            cols = pl.ds(pl.multiple_of(n * 256, 256), 256)
            logits = jnp.dot(tn[rows, :], wt[:, cols], preferred_element_type=jnp.float32)
            et[rows, cols] = jnp.exp(CAP * jnp.tanh(logits / CAP))

    teacher(0)
    tw_cp.wait_recv()
    w_nat = [[column(tw2[i, b, 0:1, :]) for b in range(2)] for i in range(2)]
    g_cp = {}
    gcol = pl.ds(pl.multiple_of(p * VT, VT), VT)
    ocol = pl.ds(pl.multiple_of((1 - p) * VT, VT), VT)

    def g_send(k, i):
        region = g_all.at[pl.ds(k * 256 + i * 128, 128), gcol]
        g_cp[k, i] = rcopy(region, region, partner)

    for k in range(2):
        for cp in z_cp[k]:
            cp.wait_recv()
        if k == 0:
            pass
        if k == 1:
            pass
        for i in range(2):
            rows = pl.ds(k * 256 + i * 128, 128)

            @pl.loop(0, 8)
            def _(n):
                cols = pl.ds(pl.multiple_of(n * 128, 128), 128)
                th_ = jnp.tanh((zo[rows, cols] + decode(zr[rows, cols])) / CAP)
                zo[rows, cols] = jnp.exp(CAP * th_)
                slope[rows, cols] = 1.0 - th_ * th_

            ar_s[k, i : i + 1, :] = row_sums(zo[rows, :])
            ar_s[k, 2 + i : 3 + i, :] = row_sums(et[rows, :])
        ar_s[k, 4:8, :] = jnp.zeros((4, 128), jnp.float32)
        if k == 0:
            pass
        rcopy(ar_s.at[k], ar_c.at[k], sibling).wait_recv()
        me_xz = x * 4 + z
        ar_r[k, me_xz] = ar_s[k] + ar_c[k]
        ar_cp = []
        for a, b in plane[1:]:
            mine = ar_r.at[k, me_xz]
            ar_cp.append(rcopy(mine, mine, dev(p, xs[a], c, h, zs_[b])))
        if k == 0:
            teacher(1)
        for cp in ar_cp:
            cp.wait_recv()
        if k == 0:
            pass
        ar_y[k, y] = jnp.sum(ar_r[k], axis=0)
        mine = ar_y.at[k, y]
        ar_cp = [rcopy(mine, mine, ydev[d]) for d in (1, 2, 3)]
        if k == 1:
            g_send(0, 1)
        for cp in ar_cp:
            cp.wait_recv()
        total = jnp.sum(ar_y[k], axis=0)
        if k == 0:
            pass
        if k == 1:
            pass
        for i in range(2):
            rows = pl.ds(k * 256 + i * 128, 128)
            w_col = jnp.concatenate(
                [
                    w_nat[i][b7][b6 * 64 + k * 32 + b43 * 8 :][:8]
                    for b7 in range(2)
                    for b43 in range(4)
                    for b6 in range(2)
                ],
                axis=0,
            )
            s_col = 1.0 / column(total[i : i + 1, :])
            t_col = 1.0 / column(total[2 + i : 3 + i, :])

            @pl.loop(0, 8)
            def _(n):
                cols = pl.ds(pl.multiple_of(n * 128, 128), 128)
                probs = (et[rows, cols] * t_col).astype(jnp.bfloat16).astype(jnp.float32)
                grad = w_col * (zo[rows, cols] * s_col - probs) * slope[rows, cols]
                g_all[rows, pl.ds(pl.multiple_of(p * VT + n * 128, 128), 128)] = grad.astype(jnp.bfloat16)

            if (k, i) != (0, 1):
                g_send(k, i)

    nt = (((1,), (1,)), ((), ()))

    @pl.loop(0, 7)
    def _(n):
        w_rows = pl.ds(pl.multiple_of(n * 256, 256), 256)
        dacc[:, w_rows] = lax.dot_general(g_all[:, gcol], ws[0, w_rows, :], nt, preferred_element_type=jnp.float32)

    rs_sem = counter[0]
    counter[0] += 4
    slot = x * 4 + z
    xcol = pl.ds(pl.multiple_of((1 - c) * CS, 128), CS)

    def rs_send(k, i, a, b):
        x_ = 2 * i + lax.rem(x + a, 2)
        return pltpu.make_async_remote_copy(
            src_ref=rs_s.at[k, x_, zs_[b]], dst_ref=rs_r.at[k, slot],
            send_sem=ssem.at[rs_sem + k], recv_sem=rsem.at[rs_sem + k],
            device_id=dev(p, x_, c, h, zs_[b]), device_id_type=MESH,
        )

    pieces = [(a, b) for b in range(4) for a in range(2)]

    def scatter(k, first, size):
        rows = pl.ds(k * 256 + first, size)

        @pl.loop(0, 7)
        def _(n):
            w_rows = pl.ds(pl.multiple_of(n * 256, 256), 256)
            dacc[rows, w_rows] += lax.dot_general(
                g_all[rows, ocol], ws[1, w_rows, :], nt, preferred_element_type=jnp.float32
            )

        rsib_s[rows, :] = dacc[rows, xcol].astype(jnp.bfloat16)
        rcopy(rsib_s.at[rows], rsib_r.at[rows], sibling).wait_recv()
        both = (dacc[rows, ccol] + rsib_r[rows, :].astype(jnp.float32)).astype(jnp.bfloat16)
        rs_s[k, first // 64 : (first + size) // 64] = both.reshape(size // 64, 4, 16, CS)
        for i in range(first // 128, (first + size) // 128):
            for a, b in pieces[1:]:
                rs_send(k, i, a, b).start()

            @pl.when(x // 2 != i)
            def _():
                rs_send(k, i, 0, 0).start()

            def rs_end(i=i):
                for a, b in pieces[1:]:
                    rs_send(k, i, a, b).wait_send()

                @pl.when(x // 2 != i)
                def _():
                    rs_send(k, i, 0, 0).wait_send()

            ends.append(rs_end)

    def gather_sum(k):
        rwait(rs_r.at[k, pl.ds(0, 15)], rsem.at[rs_sem + k])
        rs_r[k, slot] = rs_s[k, x, z]
        fin_s[k] = jnp.sum(rs_r[k].astype(jnp.float32), axis=0)
        own = fin_s.at[k, pl.ds(pl.multiple_of(c * 8, 8), 8)]
        other = fin_s.at[k, pl.ds(pl.multiple_of((1 - c) * 8, 8), 8)]

        def f_copy(n, src, device):
            return pltpu.make_async_remote_copy(
                src_ref=src, dst_ref=fin.at[c, h], send_sem=ssem.at[fin_sem + n], recv_sem=rsem.at[fin_sem + n],
                device_id=device, device_id_type=MESH,
            )

        @pl.when(h == k)
        def _():
            fin[c, h] = own[...]
            f_copy(0, other, sibling).start()

        @pl.when(h != k)
        def _():
            f_copy(1, own, hdev).start()
            f_copy(2, other, cross).start()

        def f_end():
            @pl.when(h == k)
            def _():
                f_copy(0, other, sibling).wait_send()

            @pl.when(h != k)
            def _():
                f_copy(1, own, hdev).wait_send()
                f_copy(2, other, cross).wait_send()

        ends.append(f_end)

    fin_sem = counter[0]
    counter[0] += 3
    g_cp[0, 0].wait_recv()
    g_cp[0, 1].wait_recv()
    scatter(0, 0, 256)
    g_cp[1, 0].wait_recv()
    scatter(1, 0, 128)
    gather_sum(0)
    g_cp[1, 1].wait_recv()
    scatter(1, 128, 128)
    g_out_cp = pltpu.make_async_copy(g_all, g_out, lsem.at[4])
    g_out_cp.start()
    ends.append(g_out_cp.wait)

    gather_sum(1)
    for n in range(3):
        rwait(fin.at[0, 0], rsem.at[fin_sem + n])
    scaled = jnp.concatenate([fin[0, 0] + fin[0, 1], fin[1, 0] + fin[1, 1]], axis=-1) * gain
    inn[0] = jnp.broadcast_to(jnp.sum(sx * scaled, axis=-1, keepdims=True), (8, 128))
    rcopy(inn.at[0], inn.at[1], partner).wait_recv()
    inner = (inn[0] + inn[1])[:, :1]
    dh_out[...] = stud_r * scaled - sx * (stud_r * stud_r * stud_r) * inner / DS

    finish()


def head(th, tg, sh, sg, tw, wt, ws):
    f32, bf16 = jnp.float32, jnp.bfloat16
    vmem = pl.BlockSpec(memory_space=pltpu.VMEM)
    hbm = pl.BlockSpec(memory_space=pl.ANY)
    scratch = [
        pltpu.VMEM((DT, VT), bf16),
        pltpu.VMEM((2, HS, VT), bf16),
        pltpu.VMEM((16, KT), f32),
        pltpu.VMEM((2, 4, 4, 4, 16, KT), bf16),
        pltpu.VMEM((512, DT), bf16),
        pltpu.VMEM((2, 8, 128), f32),
        pltpu.VMEM((2, 8, CS), f32),
        pltpu.VMEM((16, CS), f32),
        pltpu.VMEM((2, 4, 4, 16, HS), bf16),
        pltpu.VMEM((HS, 512), bf16),
        pltpu.VMEM((512, VT), bf16),
        pltpu.VMEM((512, VT), bf16),
        pltpu.VMEM((512, VT), f32),
        pltpu.VMEM((512, VT), f32),
        pltpu.VMEM((512, VT), f32),
        pltpu.VMEM((512, 2 * VT), bf16),
        pltpu.VMEM((2, 2, 8, 128), f32),
        pltpu.VMEM((2, 8, 128), f32),
        pltpu.VMEM((2, 8, 128), f32),
        pltpu.VMEM((2, 16, 8, 128), f32),
        pltpu.VMEM((2, 4, 8, 128), f32),
        pltpu.VMEM((512, HS), f32),
        pltpu.VMEM((512, CS), bf16),
        pltpu.VMEM((512, CS), bf16),
        pltpu.VMEM((2, 4, 4, 16, CS), bf16),
        pltpu.VMEM((2, 16, 16, CS), bf16),
        pltpu.VMEM((2, 16, CS), f32),
        pltpu.VMEM((2, 2, 8, CS), f32),
        pltpu.VMEM((2, 8, 128), f32),
        pltpu.SemaphoreType.DMA((144,)),
        pltpu.SemaphoreType.DMA((144,)),
        pltpu.SemaphoreType.DMA((5,)),
    ]
    return pl.pallas_call(
        head_kernel,
        out_shape=(
            jax.ShapeDtypeStruct((8, HS), f32),
            jax.ShapeDtypeStruct((HS, 512), bf16),
            jax.ShapeDtypeStruct((512, 2 * VT), bf16),
        ),
        in_specs=[vmem] * 5 + [hbm] * 2,
        out_specs=(vmem, hbm, hbm),
        scratch_shapes=scratch,
        compiler_params=pltpu.CompilerParams(
            collective_id=0, has_side_effects=True, vmem_limit_bytes=58 * 1024 * 1024
        ),
        name="head",
    )(th, tg, sh, sg, tw, wt, ws)


def weight_kernel(s_ref, g_ref, o_ref):
    o_ref[...] = jnp.dot(s_ref[...], g_ref[...], preferred_element_type=jnp.float32).astype(jnp.bfloat16)


def per_device(
    teacher_hidden,
    teacher_gain,
    teacher_weight,
    student_hidden,
    student_gain,
    student_weight,
    token_weight,
):
    d_hidden, s_all, g_all = head(
        teacher_hidden,
        teacher_gain,
        student_hidden,
        student_gain,
        token_weight,
        teacher_weight.reshape(DT, VT),
        student_weight,
    )
    d_weight = pl.pallas_call(
        weight_kernel,
        grid=(HS // 256,),
        in_specs=[pl.BlockSpec((256, 512), lambda i: (i, 0)), pl.BlockSpec((512, 2 * VT), lambda i: (0, 0))],
        out_specs=pl.BlockSpec((256, 2 * VT), lambda i: (i, 0)),
        out_shape=jax.ShapeDtypeStruct((HS, 2 * VT), jnp.bfloat16),
        compiler_params=pltpu.CompilerParams(vmem_limit_bytes=32 * 1024 * 1024),
        name="d_weight",
    )(s_all, g_all)
    return (d_hidden, d_weight)


def solution(mesh):
    return jax.shard_map(
        per_device,
        mesh=mesh,
        in_specs=(
            P(("pair", "vocab", "tok"), None),
            P(),
            P(None, ("vocab", "tok"), "pair", None),
            P(("vocab", "tok"), "pair"),
            P("pair"),
            P("pair", ("vocab", "tok")),
            P("pair"),
        ),
        out_specs=(P(("vocab", "tok"), "pair"), P("pair", ("vocab", "tok"))),
        check_vma=False,
    )
```

time: 142 us -> 118 us (0.83)
  Pallas kernels: 126 us -> 112 us
  matrix products: 9.22 us -> 0 us
    pallas_call x1, Pallas kernels: 126 us -> 106 us  [head(): pl.pallas_call(head_kernel, out_shape=(jax.ShapeDtypeStruct((8, HS), f32)...]
    dot_general x1 -> x0, matrix products: 9.22 us -> none  [per_device(): lax.dot_general(s_all, g_all, (((0,), (0,)), ((), ())), preferred_element...]
    pallas_call x0 -> x1, Pallas kernels: none -> 6.73 us  [per_device(): pl.pallas_call(weight_kernel, grid=(HS // 256,), in_specs=[pl.BlockSpec((...]
    reshape x4 -> x0, local copies, waits for them, and re-layouts: 3.5 us -> none  [the longest x1 1.35 us: per_device(): teacher_gain.reshape(1, DT)]
    unnamed x3 -> x7, local copies, waits for them, and re-layouts: 0.63 us -> 3.71 us
where the time goes in v2:
time: 118 us; the launch traced here: 117 us
  Pallas kernels  112 us (95%)
  local copies, waits for them, and re-layouts  3.71 us (3%)
    pallas_call x1, Pallas kernels, head(): pl.pallas_call(head_kernel, out_shape=(jax.ShapeDtypeStruct((8, HS), f32)...  106 us
    pallas_call x1, Pallas kernels, per_device(): pl.pallas_call(weight_kernel, grid=(HS // 256,), in_specs=[pl.BlockSpec((...  6.73 us
    unnamed x7, local copies, waits for them, and re-layouts  3.71 us

profile of v2, /device:TPU:31, one launch (start us, length us, event | category | flops | bytes accessed | tf_op | source)
XLA Modules:
  0.0 116.7 jit_solution(15402322697229762013)
XLA Ops:
  0.6 105.6 %head.1 = (f32[8,1792]{1,0:T(8,128)}, bf16[1792,512]{1,0:T(8,128)(2,1)}, bf16[512,2048]{1,0:T(8,128)(2,1)}) custom-call(bf16[4,4608]{1,0:T(4,128)(2,1)} %th.1, f32[4608]{0:T(1024)} %tg.1, bf16[8,1792]{1,0:T(8,128)(2,1)} %sh.1, f32[1792]{0:T(1024)} %sg.1, f32[256]{0:T(256)} %tw.1, bf16[4608,1024]{1,0:T(8,128)(2,1)} %bitcast.1, bf16[1792,2048]{1,0:T(8,128)(2,1)} %ws_hbm.1), custom_call_target="tpu_custom_call" | custom-call | tf_op jit(solution)/shard_map/head/pallas_call | solution.py:517
  106.3 0.0 copy-start
  106.3 1.6 %copy-done = bf16[512,2048]{1,0:T(8,128)(2,1)S(1)} copy-done((bf16[512,2048]{1,0:T(8,128)(2,1)S(1)}, bf16[512,2048]{1,0:T(8,128)(2,1)}, u32[]{:S(2)}) %copy-start) | copy-done | bytes 2097176
  107.9 0.0 copy-start.1
  107.9 1.5 %copy-done.1 = bf16[1792,512]{1,0:T(8,128)(2,1)S(1)} copy-done((bf16[1792,512]{1,0:T(8,128)(2,1)S(1)}, bf16[1792,512]{1,0:T(8,128)(2,1)}, u32[]{:S(2)}) %copy-start.1) | copy-done | bytes 1835032
  109.4 0.0 copy-start.2
  109.4 6.7 %d_weight.1 = bf16[1792,2048]{1,0:T(8,128)(2,1)} custom-call(bf16[1792,512]{1,0:T(8,128)(2,1)S(1)} %copy-done.1, bf16[512,2048]{1,0:T(8,128)(2,1)S(1)} %copy-done), custom_call_target="tpu_custom_call" | custom-call | tf_op jit(solution)/shard_map/d_weight/pallas_call | solution.py:556
  116.1 0.0 copy-done.2
  116.1 0.6 copy.10
Async XLA Ops:
  106.3 1.6 %copy-start = (bf16[512,2048]{1,0:T(8,128)(2,1)S(1)}, bf16[512,2048]{1,0:T(8,128)(2,1)}, u32[]{:S(2)}) copy-start(bf16[512,2048]{1,0:T(8,128)(2,1)} %get-tuple-element.7.g_ref) | copy-start | bytes 6291460
  107.9 1.5 %copy-start.1 = (bf16[1792,512]{1,0:T(8,128)(2,1)S(1)}, bf16[1792,512]{1,0:T(8,128)(2,1)}, u32[]{:S(2)}) copy-start(bf16[1792,512]{1,0:T(8,128)(2,1)} %get-tuple-element.6.s_ref) | copy-start | bytes 5505028
  109.4 6.7 %copy-start.2 = (f32[8,1792]{1,0:T(8,128)S(1)}, f32[8,1792]{1,0:T(8,128)}, u32[]{:S(2)}) copy-start(f32[8,1792]{1,0:T(8,128)} %get-tuple-element.10) | copy-start | bytes 172036

commit v3 on v2

--- a/solution.py
+++ b/solution.py
@@ -54,8 +54,8 @@
 
 def head_kernel(
     th, tg, sh, sg, tw, wt_hbm, ws_hbm,
-    dh_out, s_out, g_out,
-    wt, ws, tsc, tb, tn, sq, nf, stile, s_all, st, zs, zr, zo, slope, et, g_all, tw2,
+    dh_out, st_out, g_out, dw_own,
+    wt, ws, tsc, tb, tn, sq, nf, raw, s_all, st, zs, zr, zo, slope, et, g_all, tw2,
     ar_s, ar_c, ar_r, ar_y, dacc, rsib_s, rsib_r, rs_s, rs_r, fin_s, fin, inn,
     ssem, rsem, lsem,
 ):
@@ -78,6 +78,12 @@
     ydev = [dev(lax.rem(ys[d], 2), x, c, ys[d] // 2, z) for d in range(4)]
     hdev = ydev[2]
     cross = dev(p, x, 1 - c, 1 - h, z)
+    group = [
+        dev(1 - p if a else p, x, 1 - c if b else c, 1 - h if e else h, z)
+        for a in range(2)
+        for b in range(2)
+        for e in range(2)
+    ]
     plane = [(a, b) for b in range(4) for a in range(4)]
 
     counter = [0]
@@ -135,13 +141,17 @@
     ends.append(w_wait)
 
     bar = pltpu.get_barrier_semaphore()
-    for d in [sibling, ydev[1], ydev[2], ydev[3], cross]:
+    for d in group[1:]:
         pl.semaphore_signal(bar, inc=1, device_id=d, device_id_type=MESH)
     for a, b in plane[1:]:
         pl.semaphore_signal(bar, inc=1, device_id=dev(p, xs[a], c, h, zs_[b]), device_id_type=MESH)
 
     sx = sh[...].astype(jnp.float32)
-    sq[0] = jnp.broadcast_to(jnp.sum(sx * sx, axis=-1, keepdims=True), (8, 128))
+    sq[p, c, h] = jnp.broadcast_to(jnp.sum(sx * sx, axis=-1, keepdims=True), (8, 128))
+    nf[0] = sx[:, :CS]
+    nf[1] = sx[:, CS:]
+    mine = raw.at[h, pl.ds(pl.multiple_of(c * 8, 8), 8)]
+    mine[...] = nf[c]
     tx = th[...].astype(jnp.float32)
     tnorm = tx * lax.rsqrt(jnp.mean(tx * tx, axis=-1, keepdims=True) + EPS) * tg[...].reshape(1, DT)
     for j in range(4):
@@ -150,28 +160,29 @@
     for b in range(2):
         tw2[p, b] = jnp.broadcast_to(tw[pl.ds(128 * b, 128)].reshape(1, 128), (8, 128))
 
-    pl.semaphore_wait(bar, 20)
-
-    sq_cp = rcopy(sq.at[0], sq.at[1], partner)
-    tw_cp = rcopy(tw2.at[p], tw2.at[p], partner)
+    pl.semaphore_wait(bar, 22)
+
+    first = [
+        rcopy(nf.at[1 - c], mine, sibling),
+        rcopy(nf.at[c], mine, hdev),
+        rcopy(nf.at[1 - c], mine, cross),
+    ]
+    first += [rcopy(sq.at[p, c, h], sq.at[p, c, h], d) for d in group[1:]]
     own_t = tb.at[c, y, x, z]
     t1 = [rcopy(own_t, own_t, ydev[d]) for d in (1, 2, 3)]
-
-    sq_cp.wait_recv()
-    stud_r = lax.rsqrt((sq[0] + sq[1])[:, :1] / DS + EPS)
+    tw_cp = rcopy(tw2.at[p], tw2.at[p], partner)
     gain = sg[...].reshape(1, HS)
-    snorm = sx * stud_r * gain
-    nf[0] = snorm[:, :CS]
-    nf[1] = snorm[:, CS:]
-    mine = stile.at[pl.ds(pl.multiple_of(c * 8, 8), 8)]
-    n_cp = rcopy(nf.at[1 - c], mine, sibling)
-    mine[...] = nf[c]
-    n_cp.wait_recv()
+    gain_c = jnp.where(c == 0, gain[:, :CS], gain[:, CS:])
     ccol = pl.ds(pl.multiple_of(c * CS, 128), CS)
-    s_all[h, x, z, :, ccol] = stile[...].astype(jnp.bfloat16)
-    own_s = s_all.at[h, x, z, :, ccol]
-    h_cp = rcopy(own_s, own_s, hdev)
-    h_cp.wait_recv()
+    for cp in first:
+        cp.wait_recv()
+    for h_ in range(2):
+        tile = []
+        for c_ in range(2):
+            scale = lax.rsqrt((sq[0, c_, h_] + sq[1, c_, h_])[:, :1] / DS + EPS)
+            tile.append(raw[h_, 8 * c_ : 8 * c_ + 8] * scale * gain_c)
+        s_all[h_, x, z, :, ccol] = jnp.concatenate(tile, axis=0).astype(jnp.bfloat16)
+    stud_r = lax.rsqrt((sq[0, c, h] + sq[1, c, h])[:, :1] / DS + EPS)
     s2 = []
     for d in (1, 2, 3):
         a, b = s_all.at[0, x, z, :, ccol], s_all.at[1, x, z, :, ccol]
@@ -193,11 +204,12 @@
         s3.append(rcopy(b, b, xdev[d]))
     for cp in t2:
         cp.wait_recv()
-    t3 = []
-    for d in (1, 2, 3):
-        a, b = tb.at[c, pl.ds(0, 2), :, z], tb.at[c, pl.ds(2, 2), x]
-        t3.append(rcopy(a, a, zdev[d]))
-        t3.append(rcopy(b, b, xdev[d]))
+    t3 = ([], [])
+    for i in range(2):
+        for d in (1, 2, 3):
+            a, b = tb.at[c, i, :, z], tb.at[c, 2 + i, x]
+            t3[i].append(rcopy(a, a, zdev[d]))
+            t3[i].append(rcopy(b, b, xdev[d]))
     sib_t = []
     for r in (tb.at[c, pl.ds(0, 2), :, z], tb.at[c, pl.ds(2, 2), x]):
         sib_t.append(rcopy(r, r, sibling))
@@ -224,6 +236,16 @@
             cols = pl.ds(n * 256, 256)
             zs[rows, cols] = encode(jnp.dot(lhs, ws[1, :, cols], preferred_element_type=jnp.float32))
             z_cp[k].append(rcopy(zs.at[rows, cols], zr.at[rows, cols], partner))
+    def forward(i):
+        for d in (1, 2, 3):
+            t3[i][2 * d - 2].wait_recv()
+            r = tb.at[c, i, :, zs_[4 - d]]
+            sib_t.append(rcopy(r, r, sibling))
+            t3[i][2 * d - 1].wait_recv()
+            r = tb.at[c, 2 + i, xs[4 - d]]
+            sib_t.append(rcopy(r, r, sibling))
+
+    forward(0)
 
 
     def own_logits(k):
@@ -235,22 +257,15 @@
             zo[rows, cols] = jnp.dot(s_all[k].reshape(256, HS), ws[0, :, cols], preferred_element_type=jnp.float32)
 
     own_logits(0)
-    own_logits(1)
     for k in range(2):
         for j in range(7):
             cols = pl.ds(j * 256, 256)
             st[j * 256 : (j + 1) * 256, k * 256 : (k + 1) * 256] = s_all[k, :, :, :, cols].reshape(256, 256).T
-    s_cp = pltpu.make_async_copy(st, s_out, lsem.at[3])
-    s_cp.start()
-    ends.append(s_cp.wait)
-    for i, d in enumerate((1, 2, 3)):
-        z_, x_ = zs_[4 - d], xs[4 - d]
-        t3[2 * i].wait_recv()
-        r = tb.at[c, pl.ds(0, 2), :, z_]
-        sib_t.append(rcopy(r, r, sibling))
-        t3[2 * i + 1].wait_recv()
-        r = tb.at[c, pl.ds(2, 2), x_]
-        sib_t.append(rcopy(r, r, sibling))
+    st_cp = pltpu.make_async_copy(st, st_out, lsem.at[3])
+    st_cp.start()
+    ends.append(st_cp.wait)
+    forward(1)
+    own_logits(1)
     for cp in sib_t:
         cp.wait_recv()
 
@@ -261,7 +276,7 @@
     o_x = lax.rem(o // 8, 2)
     perm = (src == o_h * 128 + o_x * 64 + o_z * 16 + o_j * 4 + o_r).astype(jnp.bfloat16)
 
-    def teacher(k):
+    def permute(k):
         @pl.loop(4 * k, 4 * k + 4)
         def _(g):
             c_, p_, x_ = g // 4, lax.rem(g // 2, 2), lax.rem(g, 2)
@@ -271,6 +286,7 @@
             for j in range(4):
                 tn[pl.ds(pl.multiple_of(g * 64, 64), 64), j * KT : (j + 1) * KT] = out[j * 64 : (j + 1) * 64]
 
+    def teacher(k):
         rows = pl.ds(k * 256, 256)
 
         @pl.loop(0, 4)
@@ -279,6 +295,7 @@
             logits = jnp.dot(tn[rows, :], wt[:, cols], preferred_element_type=jnp.float32)
             et[rows, cols] = jnp.exp(CAP * jnp.tanh(logits / CAP))
 
+    permute(0)
     teacher(0)
     tw_cp.wait_recv()
     w_nat = [[column(tw2[i, b, 0:1, :]) for b in range(2)] for i in range(2)]
@@ -290,13 +307,11 @@
         region = g_all.at[pl.ds(k * 256 + i * 128, 128), gcol]
         g_cp[k, i] = rcopy(region, region, partner)
 
-    for k in range(2):
+    me_xz = x * 4 + z
+
+    def exps(k):
         for cp in z_cp[k]:
             cp.wait_recv()
-        if k == 0:
-            pass
-        if k == 1:
-            pass
         for i in range(2):
             rows = pl.ds(k * 256 + i * 128, 128)
 
@@ -310,64 +325,79 @@
             ar_s[k, i : i + 1, :] = row_sums(zo[rows, :])
             ar_s[k, 2 + i : 3 + i, :] = row_sums(et[rows, :])
         ar_s[k, 4:8, :] = jnp.zeros((4, 128), jnp.float32)
-        if k == 0:
-            pass
-        rcopy(ar_s.at[k], ar_c.at[k], sibling).wait_recv()
-        me_xz = x * 4 + z
+        return rcopy(ar_s.at[k], ar_c.at[k], sibling)
+
+    def to_plane(k, cp):
+        cp.wait_recv()
         ar_r[k, me_xz] = ar_s[k] + ar_c[k]
-        ar_cp = []
-        for a, b in plane[1:]:
-            mine = ar_r.at[k, me_xz]
-            ar_cp.append(rcopy(mine, mine, dev(p, xs[a], c, h, zs_[b])))
-        if k == 0:
-            teacher(1)
-        for cp in ar_cp:
+        mine = ar_r.at[k, me_xz]
+        return [rcopy(mine, mine, dev(p, xs[a], c, h, zs_[b])) for a, b in plane[1:]]
+
+    def to_column(k, cps):
+        for cp in cps:
             cp.wait_recv()
-        if k == 0:
-            pass
         ar_y[k, y] = jnp.sum(ar_r[k], axis=0)
         mine = ar_y.at[k, y]
-        ar_cp = [rcopy(mine, mine, ydev[d]) for d in (1, 2, 3)]
-        if k == 1:
-            g_send(0, 1)
-        for cp in ar_cp:
+        return [rcopy(mine, mine, ydev[d]) for d in (1, 2, 3)]
+
+    def total(k, cps):
+        for cp in cps:
             cp.wait_recv()
-        total = jnp.sum(ar_y[k], axis=0)
-        if k == 0:
-            pass
-        if k == 1:
-            pass
-        for i in range(2):
-            rows = pl.ds(k * 256 + i * 128, 128)
-            w_col = jnp.concatenate(
-                [
-                    w_nat[i][b7][b6 * 64 + k * 32 + b43 * 8 :][:8]
-                    for b7 in range(2)
-                    for b43 in range(4)
-                    for b6 in range(2)
-                ],
-                axis=0,
+        return jnp.sum(ar_y[k], axis=0)
+
+    def grads(k, i, totals):
+        rows = pl.ds(k * 256 + i * 128, 128)
+        w_col = jnp.concatenate(
+            [
+                w_nat[i][b7][b6 * 64 + k * 32 + b43 * 8 :][:8]
+                for b7 in range(2)
+                for b43 in range(4)
+                for b6 in range(2)
+            ],
+            axis=0,
+        )
+        s_col = 1.0 / column(totals[i : i + 1, :])
+        t_col = 1.0 / column(totals[2 + i : 3 + i, :])
+
+        @pl.loop(0, 8)
+        def _(n):
+            cols = pl.ds(pl.multiple_of(n * 128, 128), 128)
+            probs = (et[rows, cols] * t_col).astype(jnp.bfloat16).astype(jnp.float32)
+            grad = w_col * (zo[rows, cols] * s_col - probs) * slope[rows, cols]
+            g_all[rows, pl.ds(pl.multiple_of(p * VT + n * 128, 128), 128)] = grad.astype(jnp.bfloat16)
+
+    sib0 = exps(0)
+    plane0 = to_plane(0, sib0)
+    permute(1)
+    column0 = to_column(0, plane0)
+    teacher(1)
+    sib1 = exps(1)
+    totals = total(0, column0)
+    grads(0, 0, totals)
+    g_send(0, 0)
+    plane1 = to_plane(1, sib1)
+    grads(0, 1, totals)
+    column1 = to_column(1, plane1)
+    g_send(0, 1)
+    totals = total(1, column1)
+    for i in range(2):
+        grads(1, i, totals)
+        g_send(1, i)
+
+    nt = (((1,), (1,)), ((), ()))
+
+    def own_grad(k):
+        rows = pl.ds(k * 256, 256)
+
+        @pl.loop(0, 7)
+        def _(n):
+            w_rows = pl.ds(pl.multiple_of(n * 256, 256), 256)
+            dacc[rows, w_rows] = lax.dot_general(
+                g_all[rows, gcol], ws[0, w_rows, :], nt, preferred_element_type=jnp.float32
             )
-            s_col = 1.0 / column(total[i : i + 1, :])
-            t_col = 1.0 / column(total[2 + i : 3 + i, :])
-
-            @pl.loop(0, 8)
-            def _(n):
-                cols = pl.ds(pl.multiple_of(n * 128, 128), 128)
-                probs = (et[rows, cols] * t_col).astype(jnp.bfloat16).astype(jnp.float32)
-                grad = w_col * (zo[rows, cols] * s_col - probs) * slope[rows, cols]
-                g_all[rows, pl.ds(pl.multiple_of(p * VT + n * 128, 128), 128)] = grad.astype(jnp.bfloat16)
-
-            if (k, i) != (0, 1):
-                g_send(k, i)
-
-    nt = (((1,), (1,)), ((), ()))
-
-    @pl.loop(0, 7)
-    def _(n):
-        w_rows = pl.ds(pl.multiple_of(n * 256, 256), 256)
-        dacc[:, w_rows] = lax.dot_general(g_all[:, gcol], ws[0, w_rows, :], nt, preferred_element_type=jnp.float32)
-
+
+    own_grad(0)
+    own_grad(1)
     rs_sem = counter[0]
     counter[0] += 4
     slot = x * 4 + z
@@ -455,15 +485,23 @@
     g_cp[0, 0].wait_recv()
     g_cp[0, 1].wait_recv()
     scatter(0, 0, 256)
+
+    @pl.loop(0, 7)
+    def _(n):
+        rows = pl.ds(pl.multiple_of(n * 256, 256), 256)
+        wt[rows, :] = jnp.dot(st[rows, :], g_all[:, gcol], preferred_element_type=jnp.float32).astype(jnp.bfloat16)
+
+    dw_cp = pltpu.make_async_copy(wt.at[pl.ds(0, HS)], dw_own, lsem.at[5])
+    dw_cp.start()
+    ends.append(dw_cp.wait)
     g_cp[1, 0].wait_recv()
     scatter(1, 0, 128)
-    gather_sum(0)
     g_cp[1, 1].wait_recv()
     scatter(1, 128, 128)
-    g_out_cp = pltpu.make_async_copy(g_all, g_out, lsem.at[4])
+    gather_sum(0)
+    g_out_cp = pltpu.make_async_copy(g_all.at[:, ocol], g_out, lsem.at[4])
     g_out_cp.start()
     ends.append(g_out_cp.wait)
-
     gather_sum(1)
     for n in range(3):
         rwait(fin.at[0, 0], rsem.at[fin_sem + n])
@@ -486,9 +524,9 @@
         pltpu.VMEM((16, KT), f32),
         pltpu.VMEM((2, 4, 4, 4, 16, KT), bf16),
         pltpu.VMEM((512, DT), bf16),
-        pltpu.VMEM((2, 8, 128), f32),
+        pltpu.VMEM((2, 2, 2, 8, 128), f32),
         pltpu.VMEM((2, 8, CS), f32),
-        pltpu.VMEM((16, CS), f32),
+        pltpu.VMEM((2, 16, CS), f32),
         pltpu.VMEM((2, 4, 4, 16, HS), bf16),
         pltpu.VMEM((HS, 512), bf16),
         pltpu.VMEM((512, VT), bf16),
@@ -512,17 +550,18 @@
         pltpu.VMEM((2, 8, 128), f32),
         pltpu.SemaphoreType.DMA((144,)),
         pltpu.SemaphoreType.DMA((144,)),
-        pltpu.SemaphoreType.DMA((5,)),
+        pltpu.SemaphoreType.DMA((6,)),
     ]
     return pl.pallas_call(
         head_kernel,
         out_shape=(
             jax.ShapeDtypeStruct((8, HS), f32),
             jax.ShapeDtypeStruct((HS, 512), bf16),
-            jax.ShapeDtypeStruct((512, 2 * VT), bf16),
+            jax.ShapeDtypeStruct((512, VT), bf16),
+            jax.ShapeDtypeStruct((HS, VT), bf16),
         ),
         in_specs=[vmem] * 5 + [hbm] * 2,
-        out_specs=(vmem, hbm, hbm),
+        out_specs=(vmem, hbm, hbm, hbm),
         scratch_shapes=scratch,
         compiler_params=pltpu.CompilerParams(
             collective_id=0, has_side_effects=True, vmem_limit_bytes=58 * 1024 * 1024
@@ -531,8 +570,53 @@
     )(th, tg, sh, sg, tw, wt, ws)
 
 
-def weight_kernel(s_ref, g_ref, o_ref):
-    o_ref[...] = jnp.dot(s_ref[...], g_ref[...], preferred_element_type=jnp.float32).astype(jnp.bfloat16)
+def weight_kernel(dh_ref, own_hbm, st_hbm, g_hbm, dh_out, dw_out, st, g, own, other, in_sem, out_sem):
+    p = lax.axis_index("pair")
+    blocks = [pl.ds(256 * i, 256) for i in range(7)]
+    own_cols = pl.ds(pl.multiple_of(p * VT, VT), VT)
+    other_cols = pl.ds(pl.multiple_of((1 - p) * VT, VT), VT)
+    g_in = pltpu.make_async_copy(g_hbm, g, in_sem.at[0])
+    st_in = [pltpu.make_async_copy(st_hbm.at[b], st.at[b], in_sem.at[1 + i]) for i, b in enumerate(blocks)]
+    own_in = [pltpu.make_async_copy(own_hbm.at[b], own.at[b], in_sem.at[8 + i]) for i, b in enumerate(blocks)]
+    for cp in [g_in, *st_in, *own_in]:
+        cp.start()
+    dh_out[...] = dh_ref[...]
+    g_in.wait()
+    done = []
+    for i, b in enumerate(blocks):
+        st_in[i].wait()
+        other[b, :] = jnp.dot(st[b, :], g[...], preferred_element_type=jnp.float32).astype(jnp.bfloat16)
+        done.append(pltpu.make_async_copy(other.at[b], dw_out.at[b, other_cols], out_sem.at[i]))
+        done[-1].start()
+        own_in[i].wait()
+        done.append(pltpu.make_async_copy(own.at[b], dw_out.at[b, own_cols], out_sem.at[7 + i]))
+        done[-1].start()
+    for cp in done:
+        cp.wait()
+
+
+def finish_weight(d_hidden, own, st, g):
+    vmem = pl.BlockSpec(memory_space=pltpu.VMEM)
+    hbm = pl.BlockSpec(memory_space=pl.ANY)
+    return pl.pallas_call(
+        weight_kernel,
+        out_shape=(
+            jax.ShapeDtypeStruct((8, HS), jnp.float32),
+            jax.ShapeDtypeStruct((HS, 2 * VT), jnp.bfloat16),
+        ),
+        in_specs=[vmem, hbm, hbm, hbm],
+        out_specs=(vmem, hbm),
+        scratch_shapes=[
+            pltpu.VMEM((HS, 512), jnp.bfloat16),
+            pltpu.VMEM((512, VT), jnp.bfloat16),
+            pltpu.VMEM((HS, VT), jnp.bfloat16),
+            pltpu.VMEM((HS, VT), jnp.bfloat16),
+            pltpu.SemaphoreType.DMA((15,)),
+            pltpu.SemaphoreType.DMA((14,)),
+        ],
+        compiler_params=pltpu.CompilerParams(vmem_limit_bytes=58 * 1024 * 1024),
+        name="weight",
+    )(d_hidden, own, st, g)
 
 
 def per_device(
@@ -544,7 +628,7 @@
     student_weight,
     token_weight,
 ):
-    d_hidden, s_all, g_all = head(
+    d_hidden, st, g, own = head(
         teacher_hidden,
         teacher_gain,
         student_hidden,
@@ -553,16 +637,7 @@
         teacher_weight.reshape(DT, VT),
         student_weight,
     )
-    d_weight = pl.pallas_call(
-        weight_kernel,
-        grid=(HS // 256,),
-        in_specs=[pl.BlockSpec((256, 512), lambda i: (i, 0)), pl.BlockSpec((512, 2 * VT), lambda i: (0, 0))],
-        out_specs=pl.BlockSpec((256, 2 * VT), lambda i: (i, 0)),
-        out_shape=jax.ShapeDtypeStruct((HS, 2 * VT), jnp.bfloat16),
-        compiler_params=pltpu.CompilerParams(vmem_limit_bytes=32 * 1024 * 1024),
-        name="d_weight",
-    )(s_all, g_all)
-    return (d_hidden, d_weight)
+    return finish_weight(d_hidden, own, st, g)
 
 
 def solution(mesh):

time: 118 us -> 109 us (0.924)
  Pallas kernels: 112 us -> 107 us
  local copies, waits for them, and re-layouts: 3.71 us -> 0 us
    pallas_call x1, Pallas kernels: 106 us -> 99.6 us  [head(): pl.pallas_call(head_kernel, out_shape=(jax.ShapeDtypeStruct((8, HS), f32)...]
    unnamed x7 -> x0, local copies, waits for them, and re-layouts: 3.71 us -> none
where the time goes in v3:
time: 109 us; the launch traced here: 108 us
  Pallas kernels  107 us (98%)
    pallas_call x1, Pallas kernels, head(): pl.pallas_call(head_kernel, out_shape=(jax.ShapeDtypeStruct((8, HS), f32)...  99.6 us
    pallas_call x1, Pallas kernels, finish_weight(): pl.pallas_call(weight_kernel, out_shape=(jax.ShapeDtypeStruct((8, HS), jn...  7.22 us

profile of v3, /device:TPU:31, one launch (start us, length us, event | category | flops | bytes accessed | tf_op | source)
XLA Modules:
  0.0 107.6 jit_solution(10599891372605434340)
XLA Ops:
  0.6 99.6 %head.1 = (f32[8,1792]{1,0:T(8,128)}, bf16[1792,512]{1,0:T(8,128)(2,1)}, bf16[512,1024]{1,0:T(8,128)(2,1)}, bf16[1792,1024]{1,0:T(8,128)(2,1)}) custom-call(bf16[4,4608]{1,0:T(4,128)(2,1)} %th.1, f32[4608]{0:T(1024)} %tg.1, bf16[8,1792]{1,0:T(8,128)(2,1)} %sh.1, f32[1792]{0:T(1024)} %sg.1, f32[256]{0:T(256)} %tw.1, bf16[4608,1024]{1,0:T(8,128)(2,1)} %bitcast.1, ...), custom_call_target="tpu_custom_call" | custom-call | tf_op jit(solution)/shard_map/head/pallas_call | solution.py:555
  100.2 7.2 %weight.1 = (f32[8,1792]{1,0:T(8,128)}, bf16[1792,2048]{1,0:T(8,128)(2,1)}) custom-call(f32[8,1792]{1,0:T(8,128)} %get-tuple-element.6.dh_ref, bf16[1792,1024]{1,0:T(8,128)(2,1)} %get-tuple-element.7.own_hbm, bf16[1792,512]{1,0:T(8,128)(2,1)} %get-tuple-element.8.st_hbm, bf16[512,1024]{1,0:T(8,128)(2,1)} %get-tuple-element.9.g_hbm), custom_call_target="tpu_custom_call" | custom-call | tf_op jit(solution)/shard_map/weight/pallas_call | solution.py:601

commit v4 on v3

--- a/solution.py
+++ b/solution.py
@@ -56,7 +56,7 @@
     th, tg, sh, sg, tw, wt_hbm, ws_hbm,
     dh_out, st_out, g_out, dw_own,
     wt, ws, tsc, tb, tn, sq, nf, raw, s_all, st, zs, zr, zo, slope, et, g_all, tw2,
-    ar_s, ar_c, ar_r, ar_y, dacc, rsib_s, rsib_r, rs_s, rs_r, fin_s, fin, inn,
+    ar_s, ar_c, ar_r, ar_y, dacc, rsib_s, rsib_r, rs_s, rs_r, fin_s, fin, zp, aq_s, aq_c, aq_r, aq_y, q_sum, q_col,
     ssem, rsem, lsem,
 ):
     p = lax.axis_index("pair")
@@ -96,7 +96,6 @@
                 src_ref=src, dst_ref=dst, send_sem=ssem.at[i], recv_sem=rsem.at[i],
                 device_id=device, device_id_type=MESH,
             )
-            self.cp.start()
             self.here = False
 
         def wait_recv(self):
@@ -104,10 +103,12 @@
                 self.cp.wait_recv()
             self.here = True
 
-    def rcopy(src, dst, device):
+    def rcopy(src, dst, device, start=True):
         i = counter[0]
         counter[0] += 1
         sends.append(Copy(i, src, dst, device))
+        if start:
+            sends[-1].cp.start()
         return sends[-1]
 
     def finish():
@@ -204,15 +205,38 @@
         s3.append(rcopy(b, b, xdev[d]))
     for cp in t2:
         cp.wait_recv()
-    t3 = ([], [])
-    for i in range(2):
-        for d in (1, 2, 3):
-            a, b = tb.at[c, i, :, z], tb.at[c, 2 + i, x]
-            t3[i].append(rcopy(a, a, zdev[d]))
-            t3[i].append(rcopy(b, b, xdev[d]))
     sib_t = []
     for r in (tb.at[c, pl.ds(0, 2), :, z], tb.at[c, pl.ds(2, 2), x]):
         sib_t.append(rcopy(r, r, sibling))
+    t3, t_on = [], []
+    for d in (1, 2, 3):
+        for mine, theirs, device in (
+            (tb.at[c, pl.ds(0, 2), :, z], tb.at[c, pl.ds(0, 2), :, zs_[4 - d]], zdev[d]),
+            (tb.at[c, pl.ds(2, 2), x], tb.at[c, pl.ds(2, 2), xs[4 - d]], xdev[d]),
+        ):
+            t3.append(rcopy(mine, mine, device, start=False))
+            t_on.append(rcopy(theirs, theirs, sibling, start=False))
+
+    def t3_start(core):
+        @pl.when(c == core)
+        def _():
+            for cp in t3:
+                cp.cp.start()
+
+    def t3_forward(core):
+        @pl.when(c == core)
+        def _():
+            for cp, on in zip(t3, t_on):
+                cp.cp.wait_recv()
+                on.cp.start()
+
+    def t3_sibling(core):
+        @pl.when(c == core)
+        def _():
+            for cp in sib_t + t_on:
+                cp.cp.wait_recv()
+
+    t3_start(0)
     sib_s = ([], [])
     for i in range(4):
         if i:
@@ -236,18 +260,8 @@
             cols = pl.ds(n * 256, 256)
             zs[rows, cols] = encode(jnp.dot(lhs, ws[1, :, cols], preferred_element_type=jnp.float32))
             z_cp[k].append(rcopy(zs.at[rows, cols], zr.at[rows, cols], partner))
-    def forward(i):
-        for d in (1, 2, 3):
-            t3[i][2 * d - 2].wait_recv()
-            r = tb.at[c, i, :, zs_[4 - d]]
-            sib_t.append(rcopy(r, r, sibling))
-            t3[i][2 * d - 1].wait_recv()
-            r = tb.at[c, 2 + i, xs[4 - d]]
-            sib_t.append(rcopy(r, r, sibling))
-
-    forward(0)
-
-
+        if k == 1:
+            t3_start(1)
     def own_logits(k):
         rows = pl.ds(k * 256, 256)
 
@@ -257,18 +271,9 @@
             zo[rows, cols] = jnp.dot(s_all[k].reshape(256, HS), ws[0, :, cols], preferred_element_type=jnp.float32)
 
     own_logits(0)
-    for k in range(2):
-        for j in range(7):
-            cols = pl.ds(j * 256, 256)
-            st[j * 256 : (j + 1) * 256, k * 256 : (k + 1) * 256] = s_all[k, :, :, :, cols].reshape(256, 256).T
-    st_cp = pltpu.make_async_copy(st, st_out, lsem.at[3])
-    st_cp.start()
-    ends.append(st_cp.wait)
-    forward(1)
+    t3_forward(0)
     own_logits(1)
-    for cp in sib_t:
-        cp.wait_recv()
-
+    t3_sibling(1)
     o = lax.broadcasted_iota(jnp.int32, (256, 256), 0)
     src = lax.broadcasted_iota(jnp.int32, (256, 256), 1)
     o_j, o_r = o // 64, lax.rem(o, 4)
@@ -297,6 +302,7 @@
 
     permute(0)
     teacher(0)
+    t3_forward(1)
     tw_cp.wait_recv()
     w_nat = [[column(tw2[i, b, 0:1, :]) for b in range(2)] for i in range(2)]
     g_cp = {}
@@ -318,7 +324,9 @@
             @pl.loop(0, 8)
             def _(n):
                 cols = pl.ds(pl.multiple_of(n * 128, 128), 128)
-                th_ = jnp.tanh((zo[rows, cols] + decode(zr[rows, cols])) / CAP)
+                z_ = zo[rows, cols] + decode(zr[rows, cols])
+                zp[rows, cols] = z_
+                th_ = jnp.tanh(z_ / CAP)
                 zo[rows, cols] = jnp.exp(CAP * th_)
                 slope[rows, cols] = 1.0 - th_ * th_
 
@@ -366,8 +374,23 @@
             grad = w_col * (zo[rows, cols] * s_col - probs) * slope[rows, cols]
             g_all[rows, pl.ds(pl.multiple_of(p * VT + n * 128, 128), 128)] = grad.astype(jnp.bfloat16)
 
+    nt = (((1,), (1,)), ((), ()))
+
+    def own_grad(k):
+        rows = pl.ds(k * 256, 256)
+
+        @pl.loop(0, 7)
+        def _(n):
+            w_rows = pl.ds(pl.multiple_of(n * 256, 256), 256)
+            dacc[rows, w_rows] = lax.dot_general(
+                g_all[rows, gcol], ws[0, w_rows, :], nt, preferred_element_type=jnp.float32
+            )
+
     sib0 = exps(0)
     plane0 = to_plane(0, sib0)
+    t3_sibling(0)
+    for cp in sib_t + t3 + t_on:
+        cp.here = True
     permute(1)
     column0 = to_column(0, plane0)
     teacher(1)
@@ -379,25 +402,24 @@
     grads(0, 1, totals)
     column1 = to_column(1, plane1)
     g_send(0, 1)
+    own_grad(0)
     totals = total(1, column1)
     for i in range(2):
         grads(1, i, totals)
         g_send(1, i)
 
-    nt = (((1,), (1,)), ((), ()))
-
-    def own_grad(k):
-        rows = pl.ds(k * 256, 256)
-
-        @pl.loop(0, 7)
-        def _(n):
-            w_rows = pl.ds(pl.multiple_of(n * 256, 256), 256)
-            dacc[rows, w_rows] = lax.dot_general(
-                g_all[rows, gcol], ws[0, w_rows, :], nt, preferred_element_type=jnp.float32
-            )
-
-    own_grad(0)
+    for k in range(2):
+        for i in range(2):
+            rows = pl.ds(k * 256 + i * 128, 128)
+            n = 2 * k + i
+            aq_s[n : n + 1, :] = row_sums(g_all[rows, gcol].astype(jnp.float32) * zp[rows, :])
+    aq_s[4:8, :] = jnp.zeros((4, 128), jnp.float32)
+    q_sib = rcopy(aq_s, aq_c, sibling)
     own_grad(1)
+    q_sib.wait_recv()
+    aq_r[me_xz] = aq_s[...] + aq_c[...]
+    mine = aq_r.at[me_xz]
+    q_plane = [rcopy(mine, mine, dev(p, xs[a], c, h, zs_[b])) for a, b in plane[1:]]
     rs_sem = counter[0]
     counter[0] += 4
     slot = x * 4 + z
@@ -424,7 +446,11 @@
             )
 
         rsib_s[rows, :] = dacc[rows, xcol].astype(jnp.bfloat16)
-        rcopy(rsib_s.at[rows], rsib_r.at[rows], sibling).wait_recv()
+        return rcopy(rsib_s.at[rows], rsib_r.at[rows], sibling)
+
+    def tiles_out(k, first, size, cp):
+        rows = pl.ds(k * 256 + first, size)
+        cp.wait_recv()
         both = (dacc[rows, ccol] + rsib_r[rows, :].astype(jnp.float32)).astype(jnp.bfloat16)
         rs_s[k, first // 64 : (first + size) // 64] = both.reshape(size // 64, 4, 16, CS)
         for i in range(first // 128, (first + size) // 128):
@@ -484,8 +510,27 @@
     counter[0] += 3
     g_cp[0, 0].wait_recv()
     g_cp[0, 1].wait_recv()
-    scatter(0, 0, 256)
-
+    part = scatter(0, 0, 256)
+
+    g_cp[1, 0].wait_recv()
+    tiles_out(0, 0, 256, part)
+    part = scatter(1, 0, 128)
+    for cp in q_plane:
+        cp.wait_recv()
+    aq_y[y] = jnp.sum(aq_r[...], axis=0)
+    mine = aq_y.at[y]
+    q_column = [rcopy(mine, mine, ydev[d]) for d in (1, 2, 3)]
+    g_cp[1, 1].wait_recv()
+    tiles_out(1, 0, 128, part)
+    part = scatter(1, 128, 128)
+    tiles_out(1, 128, 128, part)
+    for k in range(2):
+        for j in range(7):
+            cols = pl.ds(j * 256, 256)
+            st[j * 256 : (j + 1) * 256, k * 256 : (k + 1) * 256] = s_all[k, :, :, :, cols].reshape(256, 256).T
+    st_cp = pltpu.make_async_copy(st, st_out, lsem.at[3])
+    st_cp.start()
+    ends.append(st_cp.wait)
     @pl.loop(0, 7)
     def _(n):
         rows = pl.ds(pl.multiple_of(n * 256, 256), 256)
@@ -494,22 +539,20 @@
     dw_cp = pltpu.make_async_copy(wt.at[pl.ds(0, HS)], dw_own, lsem.at[5])
     dw_cp.start()
     ends.append(dw_cp.wait)
-    g_cp[1, 0].wait_recv()
-    scatter(1, 0, 128)
-    g_cp[1, 1].wait_recv()
-    scatter(1, 128, 128)
     gather_sum(0)
     g_out_cp = pltpu.make_async_copy(g_all.at[:, ocol], g_out, lsem.at[4])
     g_out_cp.start()
     ends.append(g_out_cp.wait)
+    for cp in q_column:
+        cp.wait_recv()
+    q_sum[...] = jnp.sum(aq_y[...], axis=0)
+    q_col[...] = column(q_sum[pl.ds(2 * h + x // 2, 1), :])
+    q = q_col[pl.ds(pl.multiple_of(lax.rem(x, 2) * 64 + z * 16 + c * 8, 8), 8), :][:, :1]
     gather_sum(1)
     for n in range(3):
         rwait(fin.at[0, 0], rsem.at[fin_sem + n])
     scaled = jnp.concatenate([fin[0, 0] + fin[0, 1], fin[1, 0] + fin[1, 1]], axis=-1) * gain
-    inn[0] = jnp.broadcast_to(jnp.sum(sx * scaled, axis=-1, keepdims=True), (8, 128))
-    rcopy(inn.at[0], inn.at[1], partner).wait_recv()
-    inner = (inn[0] + inn[1])[:, :1]
-    dh_out[...] = stud_r * scaled - sx * (stud_r * stud_r * stud_r) * inner / DS
+    dh_out[...] = stud_r * scaled - sx * (stud_r * stud_r) * q / DS
 
     finish()
 
@@ -547,9 +590,15 @@
         pltpu.VMEM((2, 16, 16, CS), bf16),
         pltpu.VMEM((2, 16, CS), f32),
         pltpu.VMEM((2, 2, 8, CS), f32),
-        pltpu.VMEM((2, 8, 128), f32),
-        pltpu.SemaphoreType.DMA((144,)),
-        pltpu.SemaphoreType.DMA((144,)),
+        pltpu.VMEM((512, VT), f32),
+        pltpu.VMEM((8, 128), f32),
+        pltpu.VMEM((8, 128), f32),
+        pltpu.VMEM((16, 8, 128), f32),
+        pltpu.VMEM((4, 8, 128), f32),
+        pltpu.VMEM((8, 128), f32),
+        pltpu.VMEM((128, 128), f32),
+        pltpu.SemaphoreType.DMA((160,)),
+        pltpu.SemaphoreType.DMA((160,)),
         pltpu.SemaphoreType.DMA((6,)),
     ]
     return pl.pallas_call(

time: 109 us -> 105 us (0.963)
  Pallas kernels: 107 us -> 104 us
    pallas_call x1, Pallas kernels: 99.6 us -> 96.6 us  [head(): pl.pallas_call(head_kernel, out_shape=(jax.ShapeDtypeStruct((8, HS), f32)...]
where the time goes in v4:
time: 105 us
  Pallas kernels  104 us (99%)
    pallas_call x1, Pallas kernels, head(): pl.pallas_call(head_kernel, out_shape=(jax.ShapeDtypeStruct((8, HS), f32)...  96.6 us
    pallas_call x1, Pallas kernels, finish_weight(): pl.pallas_call(weight_kernel, out_shape=(jax.ShapeDtypeStruct((8, HS), jn...  7.22 us

profile of v4, /device:TPU:31, one launch (start us, length us, event | category | flops | bytes accessed | tf_op | source)
XLA Modules:
  0.0 104.6 jit_solution(10507096123150332956)
XLA Ops:
  0.6 96.6 %head.1 = (f32[8,1792]{1,0:T(8,128)}, bf16[1792,512]{1,0:T(8,128)(2,1)}, bf16[512,1024]{1,0:T(8,128)(2,1)}, bf16[1792,1024]{1,0:T(8,128)(2,1)}) custom-call(bf16[4,4608]{1,0:T(4,128)(2,1)} %th.1, f32[4608]{0:T(1024)} %tg.1, bf16[8,1792]{1,0:T(8,128)(2,1)} %sh.1, f32[1792]{0:T(1024)} %sg.1, f32[256]{0:T(256)} %tw.1, bf16[4608,1024]{1,0:T(8,128)(2,1)} %bitcast.1, ...), custom_call_target="tpu_custom_call" | custom-call | tf_op jit(solution)/shard_map/head/pallas_call | solution.py:604
  97.2 7.2 %weight.1 = (f32[8,1792]{1,0:T(8,128)}, bf16[1792,2048]{1,0:T(8,128)(2,1)}) custom-call(f32[8,1792]{1,0:T(8,128)} %get-tuple-element.6.dh_ref, bf16[1792,1024]{1,0:T(8,128)(2,1)} %get-tuple-element.7.own_hbm, bf16[1792,512]{1,0:T(8,128)(2,1)} %get-tuple-element.8.st_hbm, bf16[512,1024]{1,0:T(8,128)(2,1)} %get-tuple-element.9.g_hbm), custom_call_target="tpu_custom_call" | custom-call | tf_op jit(solution)/shard_map/weight/pallas_call | solution.py:650
